TPU v7x, 256 devices: a whole 4x4x8 slice. The times are simulated.
256 devices in a mesh: dom: 8 (over y, x_lo), pix: 32 (over x_hi, z, core).
Axes of the slice: x: 4 (x_hi: 2, x_lo: 2; x = x_hi * 2 + x_lo), y: 4, z: 8, core: 2. Of those that a mesh axis runs over, the one named last changes fastest.
Arguments:
- images: bfloat16 [8192, 2, 32768], P('dom', None, 'pix'), may hold values from -6 to 6
- slices: bfloat16 [8, 256, 2, 32768], P('dom', None, None, 'pix'), may hold values from -6 to 6
- class_of: int32 [8192, 1], P('dom'), may hold values from 0 to 7, as said below
- pose_of: int32 [8192], P('dom'), may hold values from 0 to 255, as said below
- group_of: int32 [8192], P('dom'), may hold values from 0 to 63
- defocus: bfloat16 [8192], P('dom'), may hold values from 0.5 to 1.5
- slot_class: int32 [8], replicated, may hold values from 0 to 7, each once
Outputs:
- whitened: float32 [64, 12], replicated
- defocus_score: float32 [8192], P('dom')
Inputs may be any that keep to these rules, and one draw needn't show every extreme that they name: Slot j of slices holds the projected slices of class slot_class[j]; every class stands in exactly one slot. `class_of`: among the 1024 particles of one device at most 192 have the same class; on every device one or two classes have exactly 192. `pose_of`: among one device's particles of one class, a pose is used a second time only after all 256 poses have been used.
All inputs are finite; a program needn't handle non-finite values.
Results may differ from a plain program's by a relative error of at most 0.0003.
Values may be sent and summed in bfloat16 or wider, within the bound.
No kernel may reach another device: no remote copies, remote signals or barrier semaphores. Data moves between devices by JAX's collectives and lax.ppermute only.
A program may use at most 128 MiB of HBM per device.

v0:
```python
import functools
import math

import jax
import jax.numpy as jnp
from jax import lax
from jax.experimental import pallas as pl
from jax.experimental.pallas import tpu as pltpu
from jax.sharding import PartitionSpec as P

BOX = 256
GROUPS = 64
ZERN = 12
PAIRS = ZERN * (ZERN + 1) // 2
PHASE_GAIN = 40.0
RIDGE = 1.0

WIDE = 256
MOMENTS = 96
RIGHT_AT = 80

SIN_POLY = (3.141592580044675, -5.167706878922935, 2.5500313772212047, -0.5980451737557255, 0.07722012821305138)
COS_POLY = (0.9999999534415752, -4.934792857330457, 4.058411894717311, -1.3318800570964462, 0.2196966127309024)

X_SWAP = [(d, d ^ 1) for d in range(8)]
Y_UP = [(d, (d + 2) % 8) for d in range(8)]
Y_DOWN = [(d, (d - 2) % 8) for d in range(8)]
CORE_SWAP = [(p, p ^ 1) for p in range(32)]
CORE_GROUPS = [[2 * m + c for m in range(16)] for c in range(2)]

F32 = jnp.float32
BF16 = jnp.bfloat16
SMEM = pl.BlockSpec(memory_space=pltpu.SMEM)
VMEM = pl.BlockSpec(memory_space=pltpu.VMEM)


def params():
    return pltpu.CompilerParams(vmem_limit_bytes=28 * 1024 * 1024)


def horner(coeffs, z):
    acc = jnp.full_like(z, coeffs[-1])
    for c in coeffs[-2::-1]:
        acc = acc * z + c
    return acc


STAGES = [(0, 4), (4, 7), (7, 8)]
NT = (((1,), (1,)), ((), ()))


def sort_kernel(place, slot_class, class_ref, pose_ref, group_ref, defocus_ref, image_ref, *refs):
    sorted_ref, perm_ref, col_ref, row_ref, count_ref, perm = refs
    parts = perm.shape[0]

    @pl.when(pl.program_id(0) == 0)
    def _():
        y0 = place[0] >> 1
        x0 = place[0] & 1
        cls = class_ref[...]
        block = jnp.zeros_like(cls)
        for slot in range(8):
            up = ((slot >> 1) - y0) & 3
            side = (slot & 1) ^ x0
            near = jnp.where(up == 3, 2, 3) + 2 * side
            at = jnp.where(up == 0, side, jnp.where(up == 2, 6 + side, near))
            block = jnp.where(cls == slot_class[slot], at, block)
        key = lax.broadcasted_iota(jnp.int32, (8, parts), 0)
        hot = jnp.where(key == block, 1.0, 0.0)
        sub = lax.broadcasted_iota(jnp.int32, (parts, parts), 0)
        lane = lax.broadcasted_iota(jnp.int32, (parts, parts), 1)
        perm[...] = jnp.where(sub < lane, 1.0, 0.0).astype(BF16)
        before = jnp.dot(hot.astype(BF16), perm[...], preferred_element_type=F32)
        total = jnp.sum(hot, axis=1, keepdims=True)
        rank = jnp.zeros((1, parts), F32)
        start = jnp.zeros((1, 1), F32)
        for k in range(8):
            rank = rank + hot[k : k + 1] * (before[k : k + 1] + start)
            start = start + total[k : k + 1]
        perm[...] = jnp.where(sub == rank.astype(jnp.int32), 1.0, 0.0).astype(BF16)
        perm_ref[...] = perm[...]
        mark = lax.broadcasted_iota(jnp.int32, (16, parts), 0)
        rows = jnp.where(mark == 0, block.astype(F32), 0.0)
        rows = jnp.where(mark == 1, pose_ref[...].astype(F32), rows)
        rows = jnp.where(mark == 2, defocus_ref[...], rows)
        rows = jnp.where(mark == 3, group_ref[...].astype(F32), rows).astype(BF16)
        col_ref[...] = lax.dot_general(perm[...], rows, NT, preferred_element_type=F32)
        row_ref[...] = lax.dot_general(rows, perm[...], NT, preferred_element_type=F32)
        for k in range(9):
            count_ref[k] = jnp.sum(jnp.where(block < k, 1.0, 0.0)).astype(jnp.int32)

    sorted_ref[...] = jnp.dot(perm[...], image_ref[...], preferred_element_type=F32).astype(BF16)


def sort_particles(place, slot_class, class_row, pose_row, group_row, defocus_row, images):
    parts, cols = images.shape
    row = pl.BlockSpec((1, parts), lambda i: (0, 0))
    return pl.pallas_call(
        sort_kernel,
        grid=(cols // 512,),
        in_specs=[SMEM, SMEM, row, row, row, row, pl.BlockSpec((parts, 512), lambda i: (0, i))],
        out_specs=[
            pl.BlockSpec((parts, 512), lambda i: (0, i)),
            pl.BlockSpec((parts, parts), lambda i: (0, 0)),
            pl.BlockSpec((parts, 16), lambda i: (0, 0)),
            pl.BlockSpec((16, parts), lambda i: (0, 0)),
            SMEM,
        ],
        out_shape=[
            jax.ShapeDtypeStruct((parts, cols), BF16),
            jax.ShapeDtypeStruct((parts, parts), BF16),
            jax.ShapeDtypeStruct((parts, 16), F32),
            jax.ShapeDtypeStruct((16, parts), F32),
            jax.ShapeDtypeStruct((9,), jnp.int32),
        ],
        scratch_shapes=[pltpu.VMEM((parts, parts), BF16)],
        compiler_params=params(),
        cost_estimate=pl.CostEstimate(
            flops=2 * parts * parts * cols, bytes_accessed=4 * parts * cols, transcendentals=0
        ),
        name="sort_particles",
    )(place, slot_class, class_row, pose_row, group_row, defocus_row, images)


def pixel_grid(first, count):
    index = first + lax.broadcasted_iota(jnp.int32, (1, count), 1)
    scale = math.sqrt(2.0) / BOX
    freq_x = (index & (BOX // 2 - 1)).astype(F32) * scale
    freq_y = ((index >> 7) - BOX // 2).astype(F32) * scale
    return freq_x, freq_y


def zernike_rows(freq_x, freq_y):
    q = freq_x * freq_x + freq_y * freq_y
    re1, im1 = freq_x, freq_y
    re2 = freq_x * freq_x - freq_y * freq_y
    im2 = 2.0 * freq_x * freq_y
    re3 = re2 * re1 - im2 * im1
    im3 = re2 * im1 + im2 * re1
    re5 = re3 * re2 - im3 * im2
    im5 = re3 * im2 + im3 * re2
    r3 = 3.0 * q - 2.0
    r5 = 10.0 * q * q - 12.0 * q + 3.0
    ro = 5.0 * q - 4.0
    return [re1, im1, r3 * re1, r3 * im1, r5 * re1, r5 * im1, re3, im3, ro * re3, ro * im3, re5, im5]


def row_range(stage, parts):
    return [(0, 768, 256), (256, parts, 256), (768, parts, 128)][stage]


def terms_kernel(stage, fill, refs):
    late = stage == 2
    refs = list(refs)
    core = refs.pop(0) if late else None
    first, counts, col_ref, row_ref = refs[:4]
    refs = refs[4:]
    if stage > 0:
        old_moments, old_grads = refs[:2]
        refs = refs[2:]
    image_ref = refs.pop(0)
    refs, work = refs[:-7], refs[-7:]
    table, image, sums, basis, pairs, table_sem, image_sem = work
    if late:
        keep_ref, send_ref, moment_ref, grad_ref, full = refs[-5:]
        pieces = refs[:-5]
    else:
        moment_ref, grad_ref, token_ref = refs[-3:]
        pieces = refs[:-3]
        token_ref[...] = jnp.zeros_like(token_ref)
    parts = col_ref.shape[0]
    pix_count = image_ref.shape[1] // 2
    kb_from, kb_to = STAGES[stage]
    row_from, row_to, tile = row_range(stage, parts)

    loads = []
    for i, (piece, src, src_col, dst, dst_col, rows, width) in enumerate(fill):
        loads.append(
            pltpu.make_async_copy(
                pieces[piece].at[pl.ds(src, rows), pl.ds(src_col, width)],
                table.at[pl.ds(dst, rows), pl.ds(dst_col, width)],
                table_sem.at[i],
            )
        )
    loads.append(
        pltpu.make_async_copy(image_ref.at[pl.ds(row_from, row_to - row_from), :], image, image_sem.at[0])
    )
    for copy in loads:
        copy.start()
    grad_ref[...] = old_grads[...] if stage > 0 else jnp.zeros_like(grad_ref)
    sums[...] = jnp.zeros_like(sums)
    freq_x, freq_y = pixel_grid(first[0], pix_count)
    q = freq_x * freq_x + freq_y * freq_y

    def lanes(v):
        return sum(v[:, 128 * i : 128 * i + 128] for i in range(v.shape[1] // 128))

    def work_on(at, rows):
        here = slice(at, at + rows)
        there = slice(at - row_from, at - row_from + rows)
        row = (col_ref[here, 0:1] * 256.0 + col_ref[here, 1:2]).astype(jnp.int32) - 256 * kb_from
        col = lax.broadcasted_iota(jnp.int32, (rows, 256 * (kb_to - kb_from)), 1)
        hot = jnp.where(col == row, 1.0, 0.0).astype(BF16)
        defocus = col_ref[here, 2:3] * (PHASE_GAIN / (2.0 * math.pi))
        group_hot = jnp.where(
            lax.broadcasted_iota(jnp.int32, (GROUPS, rows), 0) == row_ref[3:4, here].astype(jnp.int32), 1.0, 0.0
        ).astype(BF16)
        grad_sum = 0.0
        curv_sum = 0.0
        for pix in range(0, pix_count, WIDE):
            cols = slice(pix, pix + WIDE)
            other = slice(pix_count + pix, pix_count + pix + WIDE)
            proj_re = jnp.dot(hot, table[:, cols], preferred_element_type=F32)
            proj_im = jnp.dot(hot, table[:, other], preferred_element_type=F32)
            image_re = image[there, cols].astype(F32)
            image_im = image[there, other].astype(F32)
            q_sub = q[:, cols]

            turns = defocus * q_sub
            rest_turn = turns - jnp.floor(turns + 0.5)
            z = rest_turn * rest_turn
            s = rest_turn * horner(SIN_POLY, z)
            c = horner(COS_POLY, z)
            s2 = s + s
            sin_phi = s2 * c
            cos_phi = 1.0 - s2 * s

            power = proj_re * proj_re + proj_im * proj_im
            along = proj_re * image_re + proj_im * image_im
            across = proj_im * image_re - proj_re * image_im
            weight = (PHASE_GAIN * q_sub) * cos_phi
            sp = sin_phi * power
            grad_sum += lanes(weight * (sp + along))
            curv_sum += lanes(weight * weight * power)
            pred_power = sin_phi * sp
            cross = sin_phi * across

            cross_hi = cross.astype(BF16)
            cross_lo = (cross - cross_hi.astype(F32)).astype(BF16)
            sums[:, cols] += jnp.dot(group_hot, pred_power.astype(BF16), preferred_element_type=F32)
            sums[:, other] += jnp.dot(group_hot, cross_hi, preferred_element_type=F32) + jnp.dot(
                group_hot, cross_lo, preferred_element_type=F32
            )
        grad_ref[0:1, here] += jnp.sum(grad_sum.T, axis=0, keepdims=True)
        grad_ref[1:2, here] += jnp.sum(curv_sum.T, axis=0, keepdims=True)

    basis[...] = jnp.zeros_like(basis)
    for j, row in enumerate(zernike_rows(freq_x, freq_y)):
        basis[j : j + 1, :] = row
    pairs[72:80, :] = jnp.zeros((8, pix_count), F32)
    at = 0
    for j in range(ZERN):
        pairs[at : at + ZERN - j, :] = basis[j : j + 1, :] * basis[j:ZERN, :]
        at += ZERN - j

    for copy in loads:
        copy.wait()
    for at in range(row_from, row_to, tile):
        some = (counts[kb_from] < at + tile) & (counts[kb_to] > at)
        pl.when(some)(functools.partial(work_on, at, tile))

    normal = lax.dot_general(
        pairs[...], sums[:, :pix_count], NT, precision=lax.Precision.HIGHEST, preferred_element_type=F32
    )
    right = lax.dot_general(
        basis[...], sums[:, pix_count:], NT, precision=lax.Precision.HIGHEST, preferred_element_type=F32
    )
    if stage > 0:
        normal = normal + old_moments[0:RIGHT_AT, :]
        right = right + old_moments[RIGHT_AT:, :]
    moment_ref[0:RIGHT_AT, :] = normal
    moment_ref[RIGHT_AT:, :] = right

    if late:
        grads = grad_ref[...]
        moments = moment_ref[...]
        packed = jnp.concatenate([moments[: MOMENTS // 2], moments[MOMENTS // 2 :]], axis=1)
        for h in range(2):
            full[32 * h : 32 * h + 24, :] = packed[24 * h : 24 * h + 24]
            for r in range(4):
                at = 512 * h + 128 * r
                full[32 * h + 24 + r : 32 * h + 25 + r, :] = grads[0:1, at : at + 128]
                full[32 * h + 28 + r : 32 * h + 29 + r, :] = grads[1:2, at : at + 128]
        keep_ref[...] = full[pl.ds(pl.multiple_of(core[0] * 32, 32), 32), :]
        send_ref[...] = full[pl.ds(pl.multiple_of((1 - core[0]) * 32, 32), 32), :]


def particle_terms(stage, fill, first, counts, mark_cols, mark_rows, images, pieces, before=(), core=None):
    parts = mark_cols.shape[0]
    pix_count = images.shape[1] // 2
    late = stage == 2
    operands = [first, counts, mark_cols, mark_rows, *before]
    specs = [SMEM, SMEM] + [VMEM] * (2 + len(before))
    if late:
        operands = [core] + operands
        specs = [SMEM] + specs
    operands += [images, *pieces]
    specs += [pl.BlockSpec(memory_space=pltpu.HBM)] + [pl.BlockSpec(memory_space=pl.ANY)] * len(pieces)
    moments = jax.ShapeDtypeStruct((MOMENTS, GROUPS), F32)
    grads = jax.ShapeDtypeStruct((2, parts), F32)
    half = jax.ShapeDtypeStruct((32, 128), F32)
    kb_from, kb_to = STAGES[stage]
    row_from, row_to, _ = row_range(stage, parts)
    work = [
        pltpu.VMEM((256 * (kb_to - kb_from), 2 * pix_count), BF16),
        pltpu.VMEM((row_to - row_from, 2 * pix_count), BF16),
        pltpu.VMEM((GROUPS, 2 * pix_count), F32),
        pltpu.VMEM((16, pix_count), F32),
        pltpu.VMEM((RIGHT_AT, pix_count), F32),
        pltpu.SemaphoreType.DMA((len(fill),)),
        pltpu.SemaphoreType.DMA((1,)),
    ]
    if late:
        out_shape = [half, half]
        scratch = [
            pltpu.VMEM(moments.shape, F32),
            pltpu.VMEM(grads.shape, F32),
            pltpu.VMEM((64, 128), F32),
        ] + work
    else:
        out_shape = [moments, grads, jax.ShapeDtypeStruct((16, pix_count), BF16)]
        scratch = work

    def body(*refs):
        terms_kernel(stage, fill, refs)

    return pl.pallas_call(
        body,
        in_specs=specs,
        out_specs=[VMEM] * len(out_shape),
        out_shape=out_shape,
        scratch_shapes=scratch,
        compiler_params=params(),
        cost_estimate=pl.CostEstimate(
            flops=[4, 3, 1][stage] * 2 * parts * 2048 * pix_count,
            bytes_accessed=8 * 1024 * 1024,
            transcendentals=0,
        ),
        name="terms_%d" % stage,
    )(*operands)


def whiten_kernel(core, own_ref, other_ref, perm_ref, white_ref, score_ref, both, rows, perm, perm_sem, split):
    perm_load = pltpu.make_async_copy(perm_ref, perm, perm_sem.at[0])
    perm_load.start()
    both[pl.ds(pl.multiple_of(core[0] * 32, 32), 32), :] = own_ref[...]
    both[pl.ds(pl.multiple_of((1 - core[0]) * 32, 32), 32), :] = other_ref[...]
    low = jnp.concatenate([both[0:24, :], both[32:56, :]], axis=0)
    moments = jnp.concatenate([low[:, :GROUPS], low[:, GROUPS:]], axis=0)
    at = 0
    rows[...] = jnp.zeros_like(rows)
    for j in range(ZERN):
        rows[j, j:ZERN, :] = moments[at : at + ZERN - j]
        at += ZERN - j
    right = moments[RIGHT_AT : RIGHT_AT + 16]
    line = [rows[j] for j in range(ZERN)]
    lane_row = lax.broadcasted_iota(jnp.int32, (16, GROUPS), 0)
    done = jnp.zeros((16, GROUPS), F32)
    for j in range(ZERN):
        inv = lax.rsqrt(line[j][j : j + 1] + RIDGE)
        col = line[j] * inv
        value = right[j : j + 1] * inv
        done = jnp.where(lane_row == j, value, done)
        right = right - col * value
        for i in range(j + 1, ZERN):
            line[i] = line[i] - col[i : i + 1] * col
    white_ref[...] = done[:ZERN]
    split[...] = jnp.zeros_like(split)
    for h in range(2):
        grad = both[32 * h + 24 : 32 * h + 28, :]
        curv = both[32 * h + 28 : 32 * h + 32, :]
        score = -grad * lax.rsqrt(curv + 1e-06)
        for r in range(4):
            at = 512 * h + 128 * r
            rest = score[r : r + 1]
            for k in range(3):
                term = rest.astype(BF16).astype(F32)
                split[k : k + 1, at : at + 128] = term
                rest = rest - term
    perm_load.wait()
    back = jnp.dot(split[...].astype(BF16), perm[...], preferred_element_type=F32)
    score_ref[...] = back[0:1] + back[1:2] + back[2:3]


def spread(block, count):
    return jnp.broadcast_to(block[None], (count,) + block.shape)


def reduce_all(core, keep, send, perm):
    mine = keep + lax.ppermute(send, "pix", CORE_SWAP)
    moments = jnp.sum(lax.all_to_all(spread(mine[:24], 8), "dom", 0, 0), axis=0)
    mine = jnp.concatenate([moments, mine[24:]], axis=0)
    mine = jnp.sum(lax.all_to_all(spread(mine, 16), "pix", 0, 0, axis_index_groups=CORE_GROUPS), axis=0)
    other = lax.ppermute(mine, "pix", CORE_SWAP)
    white, score = pl.pallas_call(
        whiten_kernel,
        in_specs=[SMEM, VMEM, VMEM, pl.BlockSpec(memory_space=pltpu.HBM)],
        out_shape=[
            jax.ShapeDtypeStruct((ZERN, GROUPS), F32),
            jax.ShapeDtypeStruct((1, perm.shape[0]), F32),
        ],
        scratch_shapes=[
            pltpu.VMEM((64, 128), F32),
            pltpu.VMEM((ZERN, 16, GROUPS), F32),
            pltpu.VMEM(perm.shape, BF16),
            pltpu.SemaphoreType.DMA((1,)),
            pltpu.VMEM((16, perm.shape[0]), F32),
        ],
        name="whiten",
    )(core, mine, other, perm)
    return white.T, score.reshape(-1)


def hop(block, perm):
    return lax.ppermute(block, "dom", perm)


def fills(pix_count):
    half = pix_count // 2

    def parted(piece, src, dst, rows, at):
        return [(piece, src, part * half, dst, part * pix_count + at, rows, half) for part in range(2)]

    own = [(piece, 0, 0, 256 * piece, 0, 256, 2 * pix_count) for piece in range(4)]
    next_a = parted(0, 0, 0, 256, 0) + parted(1, 0, 256, 256, 0)
    next_b = parted(2, 0, 0, 512, half)
    far = parted(0, 256, 512, 128, 0) + parted(1, 256, 640, 128, 0)
    far += parted(0, 384, 512, 128, half) + parted(1, 384, 640, 128, half)
    last = parted(0, 0, 0, 128, 0) + parted(1, 0, 128, 128, 0) + parted(2, 0, 0, 256, half)
    return [own, next_a + next_b + far, last]


def local(images, slices, class_of, pose_of, group_of, defocus, slot_class):
    parts, _, pix_count = images.shape
    poses = slices.shape[1]
    dom_at = lax.axis_index("dom").astype(jnp.int32).reshape(1)
    pix_at = lax.axis_index("pix").astype(jnp.int32)
    core = (pix_at & 1).reshape(1)
    first = (pix_at * pix_count).reshape(1)
    half = pix_count // 2
    flat = slices.reshape(poses, 2 * pix_count)

    def rows(*blocks):
        return jnp.concatenate(blocks, axis=0)

    def cols(*blocks):
        return jnp.concatenate(blocks, axis=1)

    def part_a(block):
        return cols(block[:, :half], block[:, pix_count : pix_count + half])

    def part_b(block):
        return cols(block[:, half:pix_count], block[:, pix_count + half :])

    side = hop(flat, X_SWAP)
    below = hop(flat, Y_UP)
    above = hop(flat, Y_DOWN)
    image_rows, perm, mark_cols, mark_rows, counts = sort_particles(
        dom_at,
        slot_class,
        class_of.reshape(1, parts),
        pose_of[None, :],
        group_of[None, :],
        defocus.astype(F32)[None, :],
        images.reshape(parts, 2 * pix_count),
    )

    up = hop(rows(part_a(side), part_a(below[:128]), part_b(below[:128])), Y_UP)
    down = hop(rows(part_a(side), part_a(above[128:]), part_b(above[128:]), image_rows[:16, :pix_count]), Y_DOWN)
    b_side = hop(rows(part_b(below), part_b(above)), X_SWAP)
    fill = fills(pix_count)
    shared = (first, counts, mark_cols, mark_rows, image_rows)
    *sums, token = particle_terms(0, fill[0], *shared, [flat, side, below, above])

    far_a_0 = hop(up[:128], Y_UP)
    far_a_1 = hop(down[128:256], Y_DOWN)
    far_b = hop(rows(up[384:512], down[384:512], token), X_SWAP)
    *sums, _ = particle_terms(1, fill[1], *shared, [up, down, b_side], sums)
    keep, send = particle_terms(2, fill[2], *shared, [far_a_0, far_a_1, far_b], sums, core)
    return reduce_all(core, keep, send, perm)


def solution(mesh):
    return jax.shard_map(
        local,
        mesh=mesh,
        in_specs=(
            P("dom", None, "pix"),
            P("dom", None, None, "pix"),
            P("dom", None),
            P("dom"),
            P("dom"),
            P("dom"),
            P(),
        ),
        out_specs=(P(), P("dom")),
        check_vma=False,
    )
```

profile of v0, /device:TPU:1, one launch (start us, length us, event | category | flops | bytes accessed | tf_op | source)
XLA Modules:
  0.0 114.6 jit_solution(14736759046033357223)
XLA Ops:
  0.6 1.5 %copy.10 = bf16[32,8,2,1024]{3,1,2,0:T(8,128)(2,1)S(1)} copy(bf16[32,8,2,1024]{3,2,1,0:T(2,128)(2,1)} %bitcast.24) | data formatting | bytes 2097152
  2.1 2.2 %collective-permute-start.1 = (bf16[256,2048]{1,0:T(8,128)(2,1)S(1)}, bf16[256,2048]{1,0:T(8,128)(2,1)S(1)}, u32[]{:S(2)}, u32[]{:S(2)}) collective-permute-start(bf16[256,2048]{1,0:T(8,128)(2,1)S(1)} %bitcast.15), channel_id=1, source_target_pairs={{0,64},{32,96},{64,128},{96,160},{128,192},{160,224},{192,0},{224,... | collective-permute-start | bytes 3145736 | tf_op jit(solution)/shard_map/ppermute | solution.py:415
  4.3 1.2 %collective-permute-start = (bf16[256,2048]{1,0:T(8,128)(2,1)S(1)}, bf16[256,2048]{1,0:T(8,128)(2,1)}, u32[]{:S(2)}, u32[]{:S(2)}) collective-permute-start(bf16[256,2048]{1,0:T(8,128)(2,1)S(1)} %bitcast.16), channel_id=1, source_target_pairs={{0,32},{32,0},{64,96},{96,64},{128,160},{160,128},{192,224},{224,1... | collective-permute-start | bytes 3145736 | tf_op jit(solution)/shard_map/ppermute | solution.py:415
  5.6 1.5 %collective-permute-start.2 = (bf16[256,2048]{1,0:T(8,128)(2,1)S(1)}, bf16[256,2048]{1,0:T(8,128)(2,1)S(1)}, u32[]{:S(2)}, u32[]{:S(2)}) collective-permute-start(bf16[256,2048]{1,0:T(8,128)(2,1)S(1)} %bitcast.17), channel_id=1, source_target_pairs={{0,192},{32,224},{64,0},{96,32},{128,64},{160,96},{192,128},{224,1... | collective-permute-start | bytes 3145736 | tf_op jit(solution)/shard_map/ppermute | solution.py:415
  7.1 3.7 %copy.9 = bf16[128,8,2,1024]{3,1,2,0:T(8,128)(2,1)S(1)} copy(bf16[128,8,2,1024]{3,2,1,0:T(2,128)(2,1)} %bitcast.23) | data formatting | bytes 8388608
  10.9 9.5 %sort_particles.1 = (bf16[1024,2048]{1,0:T(8,128)(2,1)S(1)}, bf16[1024,1024]{1,0:T(8,128)(2,1)S(1)}, f32[1024,16]{1,0:T(8,128)S(1)}, f32[16,1024]{1,0:T(8,128)S(1)}, s32[9]{0:T(128)S(1)}) custom-call(s32[1]{0:T(128)} %bitcast.2.place, s32[8]{0:T(128)S(1)} %copy-done.4, s32[1,1024]{1,0:T(1,128)S(1)} %bitcast.20, s32[1,1024]{1,0:T(1,128)S(1)} %bitcast.21, ...), custom_call_target="tpu_custom_call" | custom-call | flops 4294967296 | bytes 8388608 | tf_op jit(solution)/shard_map/sort_particles/pallas_call | solution.py:98
  20.4 6.2 %collective-permute-done.1.refs_7_ = bf16[256,2048]{1,0:T(8,128)(2,1)S(1)} collective-permute-done((bf16[256,2048]{1,0:T(8,128)(2,1)S(1)}, bf16[256,2048]{1,0:T(8,128)(2,1)S(1)}, u32[]{:S(2)}, u32[]{:S(2)}) %collective-permute-start.1) | collective-permute-done | bytes 1048608 | tf_op jit(solution)/shard_map/ppermute | solution.py:415
  26.7 1.2 %collective-permute-done.refs_6_ = bf16[256,2048]{1,0:T(8,128)(2,1)} collective-permute-done((bf16[256,2048]{1,0:T(8,128)(2,1)S(1)}, bf16[256,2048]{1,0:T(8,128)(2,1)}, u32[]{:S(2)}, u32[]{:S(2)}) %collective-permute-start) | collective-permute-done | bytes 1048608 | tf_op jit(solution)/shard_map/ppermute | solution.py:415
  27.9 1.1 fusion.5
  29.1 1.6 %collective-permute-start.3 = (bf16[512,1024]{1,0:T(8,128)(2,1)S(1)}, bf16[512,1024]{1,0:T(8,128)(2,1)S(1)}, u32[]{:S(2)}, u32[]{:S(2)}) collective-permute-start(bf16[512,1024]{1,0:T(8,128)(2,1)S(1)} %maximum_maximum_fusion), channel_id=1, source_target_pairs={{0,64},{32,96},{64,128},{96,160},{128,192},{160,224},{192,0},{224,... | collective-permute-start | bytes 3145736 | tf_op jit(solution)/shard_map/ppermute | solution.py:415
  30.8 0.1 pad_maximum_fusion
  31.0 1.2 %collective-permute-start.4 = (bf16[528,1024]{1,0:T(8,128)(2,1)S(1)}, bf16[528,1024]{1,0:T(8,128)(2,1)S(1)}, u32[]{:S(2)}, u32[]{:S(2)}) collective-permute-start(bf16[528,1024]{1,0:T(8,128)(2,1)S(1)} %pad_maximum_fusion), channel_id=1, source_target_pairs={{0,192},{32,224},{64,0},{96,32},{128,64},{160,96},{192,128},{224,1... | collective-permute-start | bytes 3244040 | tf_op jit(solution)/shard_map/ppermute | solution.py:415
  32.2 0.1 maximum_maximum_fusion.1
  32.4 1.9 %collective-permute-start.5 = (bf16[512,1024]{1,0:T(8,128)(2,1)S(1)}, bf16[512,1024]{1,0:T(8,128)(2,1)S(1)}, u32[]{:S(2)}, u32[]{:S(2)}) collective-permute-start(bf16[512,1024]{1,0:T(8,128)(2,1)S(1)} %maximum_maximum_fusion.1), channel_id=1, source_target_pairs={{0,32},{32,0},{64,96},{96,64},{128,160},{160,128},{192,224},{224,1... | collective-permute-start | bytes 3145736 | tf_op jit(solution)/shard_map/ppermute | solution.py:415
  34.3 8.4 %terms_0.1 = (f32[96,64]{1,0:T(8,128)S(1)}, f32[2,1024]{1,0:T(2,128)S(1)}, bf16[16,1024]{1,0:T(8,128)(2,1)S(1)}) custom-call(s32[1]{0:T(128)} %bitcast.1.refs_0_.refs_1_, s32[9]{0:T(128)S(1)} %get-tuple-element.16.refs_1_.refs_2_, f32[1024,16]{1,0:T(8,128)S(1)} %get-tuple-element.17.refs_2_.refs_3_, f32[16,1024]{1,0:T(8,128)S(1)} %get-tuple-element.18.refs_3_.refs_4_, ...), custom_call_target="tpu_custom_call" | custom-call | flops 17179869184 | bytes 8388608 | tf_op jit(solution)/shard_map/terms_0/pallas_call | solution.py:327
  42.7 10.2 %collective-permute-done.3.refs_7_ = bf16[512,1024]{1,0:T(8,128)(2,1)S(1)} collective-permute-done((bf16[512,1024]{1,0:T(8,128)(2,1)S(1)}, bf16[512,1024]{1,0:T(8,128)(2,1)S(1)}, u32[]{:S(2)}, u32[]{:S(2)}) %collective-permute-start.3) | collective-permute-done | bytes 1048608 | tf_op jit(solution)/shard_map/ppermute | solution.py:415
  52.9 0.7 collective-permute-start.6
  53.7 0.6 collective-permute-done.4.refs_8_
  54.3 2.1 %collective-permute-start.7 = (bf16[128,1024]{1,0:T(8,128)(2,1)S(1)}, bf16[128,1024]{1,0:T(8,128)(2,1)S(1)}, u32[]{:S(2)}, u32[]{:S(2)}) collective-permute-start(bf16[128,1024]{1,0:T(8,128)(2,1)S(1)} %get-tuple-element.31), channel_id=1, source_target_pairs={{0,192},{32,224},{64,0},{96,32},{128,64},{160,96},{192,128},{224,1... | collective-permute-start | bytes 786440 | tf_op jit(solution)/shard_map/ppermute | solution.py:415
  56.4 2.5 %collective-permute-start.8 = (bf16[272,1024]{1,0:T(8,128)(2,1)S(1)}, bf16[272,1024]{1,0:T(8,128)(2,1)S(1)}, u32[]{:S(2)}, u32[]{:S(2)}) collective-permute-start(bf16[272,1024]{1,0:T(8,128)(2,1)S(1)} %pad_maximum_fusion.1), channel_id=1, source_target_pairs={{0,32},{32,0},{64,96},{96,64},{128,160},{160,128},{192,224},{224,1... | collective-permute-start | bytes 1671176 | tf_op jit(solution)/shard_map/ppermute | solution.py:415
  58.9 10.2 %terms_1.1 = (f32[96,64]{1,0:T(8,128)S(1)}, f32[2,1024]{1,0:T(2,128)S(1)}, bf16[16,1024]{1,0:T(8,128)(2,1)}) custom-call(s32[1]{0:T(128)} %bitcast.1.refs_0_.refs_1_, s32[9]{0:T(128)S(1)} %get-tuple-element.16.refs_1_.refs_2_, f32[1024,16]{1,0:T(8,128)S(1)} %get-tuple-element.17.refs_2_.refs_3_, f32[16,1024]{1,0:T(8,128)S(1)} %get-tuple-element.18.refs_3_.refs_4_, ...), custom_call_target="tpu_custom_call" | custom-call | flops 12884901888 | bytes 8388608 | tf_op jit(solution)/shard_map/terms_1/pallas_call | solution.py:327
  69.1 3.1 %terms_2.1 = (f32[32,128]{1,0:T(8,128)S(1)}, f32[32,128]{1,0:T(8,128)S(1)}) custom-call(s32[1]{0:T(128)} %bitcast.refs_0_.core, s32[1]{0:T(128)} %bitcast.1.refs_0_.refs_1_, s32[9]{0:T(128)S(1)} %get-tuple-element.16.refs_1_.refs_2_, f32[1024,16]{1,0:T(8,128)S(1)} %get-tuple-element.17.refs_2_.refs_3_, f32[16,1024]{1,0:T(8,128)S(1)} %get-tuple-element.18.refs_3_.refs_4_, ...), custom_call_target="tpu_custom_call" | custom-call | flops 4294967296 | bytes 8388608 | tf_op jit(solution)/shard_map/terms_2/pallas_call | solution.py:327
  72.2 3.4 %collective-permute-start.9 = (f32[32,128]{1,0:T(8,128)S(1)}, f32[32,128]{1,0:T(8,128)S(1)}, u32[]{:S(2)}, u32[]{:S(2)}) collective-permute-start(f32[32,128]{1,0:T(8,128)S(1)} %get-tuple-element.26), channel_id=1, source_target_pairs={{0,1},{1,0},{2,3},{3,2},{4,5},{5,4},{6,7},{7,6},{8,9},{9,8},{10,11... | collective-permute-start | bytes 49160 | tf_op jit(solution)/shard_map/ppermute | solution.py:390
  75.6 0.8 collective-permute-done.9
  76.5 0.6 broadcast_in_dim.27
  77.1 3.4 %all-to-all-start = ((f32[8,24,128]{2,1,0:T(8,128)}), f32[8,24,128]{2,1,0:T(8,128)S(1)}, u32[]{:S(2)}, u32[]{:S(2)}) async-start(f32[8,24,128]{2,1,0:T(8,128)} %broadcast_in_dim.27), calls=%async_computation | async-start | bytes 196608 | tf_op jit(solution)/shard_map/all_to_all | solution.py:391
  80.5 5.4 %all-to-all-done = f32[8,24,128]{2,1,0:T(8,128)S(1)} async-done(((f32[8,24,128]{2,1,0:T(8,128)}), f32[8,24,128]{2,1,0:T(8,128)S(1)}, u32[]{:S(2)}, u32[]{:S(2)}) %all-to-all-start) | async-done | bytes 98336 | tf_op jit(solution)/shard_map/all_to_all | solution.py:391
  86.0 20.1 %all_to_all.10 = f32[16,32,128]{2,1,0:T(8,128)S(1)} all-to-all(f32[16,32,128]{2,1,0:T(8,128)S(1)} %broadcast_in_dim.28), channel_id=1, replica_groups={{0,2,4,6,8,10,12,14,16,18,20,22,24,26,28,30},{1,3,5,7,9,11,13,15,17,19,..., dimensions={0} | all-to-all | bytes 524288 | tf_op jit(solution)/shard_map/all_to_all | solution.py:393
  106.1 3.6 %collective-permute-start.10 = (f32[32,128]{1,0:T(8,128)S(1)}, f32[32,128]{1,0:T(8,128)S(1)}, u32[]{:S(2)}, u32[]{:S(2)}) collective-permute-start(f32[32,128]{1,0:T(8,128)S(1)} %reduce_sum.19.own_ref), channel_id=1, source_target_pairs={{0,1},{1,0},{2,3},{3,2},{4,5},{5,4},{6,7},{7,6},{8,9},{9,8},{10,11... | collective-permute-start | bytes 49160 | tf_op jit(solution)/shard_map/ppermute | solution.py:394
  109.7 0.8 collective-permute-done.10.other_ref
  110.5 0.6 copy-done.6
  111.1 3.3 %whiten.1 = (f32[12,64]{1,0:T(8,128)}, f32[1,1024]{1,0:T(1,128)}) custom-call(s32[1]{0:T(128)} %bitcast.refs_0_.core, f32[32,128]{1,0:T(8,128)} %copy-done.5, f32[32,128]{1,0:T(8,128)} %copy-done.6, bf16[1024,1024]{1,0:T(8,128)(2,1)} %copy-done), custom_call_target="tpu_custom_call" | custom-call | tf_op jit(solution)/shard_map/whiten/pallas_call | solution.py:395
  (37 shorter events, 0.5 us)
Async XLA Ops:
  0.6 6.5 %copy-start.7 = (bf16[1024]{0:T(1024)(128)(2,1)S(1)}, bf16[1024]{0:T(1024)(128)(2,1)}, u32[]{:S(2)}) copy-start(bf16[1024]{0:T(1024)(128)(2,1)} %param.12) | copy-start | bytes 6148
  2.1 24.5 %collective-permute-start.1 = (bf16[256,2048]{1,0:T(8,128)(2,1)S(1)}, bf16[256,2048]{1,0:T(8,128)(2,1)S(1)}, u32[]{:S(2)}, u32[]{:S(2)}) collective-permute-start(bf16[256,2048]{1,0:T(8,128)(2,1)S(1)} %bitcast.15), channel_id=1, source_target_pairs={{0,64},{32,96},{64,128},{96,160},{128,192},{160,224},{192,0},{224,... | collective-permute-start | bytes 3145736 | tf_op jit(solution)/shard_map/ppermute | solution.py:415
  4.3 23.5 %collective-permute-start = (bf16[256,2048]{1,0:T(8,128)(2,1)S(1)}, bf16[256,2048]{1,0:T(8,128)(2,1)}, u32[]{:S(2)}, u32[]{:S(2)}) collective-permute-start(bf16[256,2048]{1,0:T(8,128)(2,1)S(1)} %bitcast.16), channel_id=1, source_target_pairs={{0,32},{32,0},{64,96},{96,64},{128,160},{160,128},{192,224},{224,1... | collective-permute-start | bytes 3145736 | tf_op jit(solution)/shard_map/ppermute | solution.py:415
  5.6 25.2 %collective-permute-start.2 = (bf16[256,2048]{1,0:T(8,128)(2,1)S(1)}, bf16[256,2048]{1,0:T(8,128)(2,1)S(1)}, u32[]{:S(2)}, u32[]{:S(2)}) collective-permute-start(bf16[256,2048]{1,0:T(8,128)(2,1)S(1)} %bitcast.17), channel_id=1, source_target_pairs={{0,192},{32,224},{64,0},{96,32},{128,64},{160,96},{192,128},{224,1... | collective-permute-start | bytes 3145736 | tf_op jit(solution)/shard_map/ppermute | solution.py:415
  7.1 3.7 %copy-start.1 = (s32[1024,1]{0,1:T(1,128)S(1)}, s32[1024,1]{0,1:T(1,128)}, u32[]{:S(2)}) copy-start(s32[1024,1]{0,1:T(1,128)} %param.9) | copy-start | bytes 12292
  7.1 3.7 %copy-start.2 = (s32[1024]{0:T(1024)S(1)}, s32[1024]{0:T(1024)}, u32[]{:S(2)}) copy-start(s32[1024]{0:T(1024)} %param.10) | copy-start | bytes 12292
  7.1 3.7 %copy-start.3 = (s32[1024]{0:T(1024)S(1)}, s32[1024]{0:T(1024)}, u32[]{:S(2)}) copy-start(s32[1024]{0:T(1024)} %param.11) | copy-start | bytes 12292
  7.1 3.7 %copy-start.4 = (s32[8]{0:T(128)S(1)}, s32[8]{0:T(128)}, u32[]{:S(2)}) copy-start(s32[8]{0:T(128)} %slot_class.1) | copy-start | bytes 100
  20.4 8.7 %copy-start = (bf16[1024,1024]{1,0:T(8,128)(2,1)}, bf16[1024,1024]{1,0:T(8,128)(2,1)S(1)}, u32[]{:S(2)}) copy-start(bf16[1024,1024]{1,0:T(8,128)(2,1)S(1)} %get-tuple-element.27.perm_ref) | copy-start | bytes 6291460
  29.1 23.8 %collective-permute-start.3 = (bf16[512,1024]{1,0:T(8,128)(2,1)S(1)}, bf16[512,1024]{1,0:T(8,128)(2,1)S(1)}, u32[]{:S(2)}, u32[]{:S(2)}) collective-permute-start(bf16[512,1024]{1,0:T(8,128)(2,1)S(1)} %maximum_maximum_fusion), channel_id=1, source_target_pairs={{0,64},{32,96},{64,128},{96,160},{128,192},{160,224},{192,0},{224,... | collective-permute-start | bytes 3145736 | tf_op jit(solution)/shard_map/ppermute | solution.py:415
  31.0 23.3 %collective-permute-start.4 = (bf16[528,1024]{1,0:T(8,128)(2,1)S(1)}, bf16[528,1024]{1,0:T(8,128)(2,1)S(1)}, u32[]{:S(2)}, u32[]{:S(2)}) collective-permute-start(bf16[528,1024]{1,0:T(8,128)(2,1)S(1)} %pad_maximum_fusion), channel_id=1, source_target_pairs={{0,192},{32,224},{64,0},{96,32},{128,64},{160,96},{192,128},{224,1... | collective-permute-start | bytes 3244040 | tf_op jit(solution)/shard_map/ppermute | solution.py:415
  32.4 26.6 %collective-permute-start.5 = (bf16[512,1024]{1,0:T(8,128)(2,1)S(1)}, bf16[512,1024]{1,0:T(8,128)(2,1)S(1)}, u32[]{:S(2)}, u32[]{:S(2)}) collective-permute-start(bf16[512,1024]{1,0:T(8,128)(2,1)S(1)} %maximum_maximum_fusion.1), channel_id=1, source_target_pairs={{0,32},{32,0},{64,96},{96,64},{128,160},{160,128},{192,224},{224,1... | collective-permute-start | bytes 3145736 | tf_op jit(solution)/shard_map/ppermute | solution.py:415
  52.9 16.2 %collective-permute-start.6 = (bf16[128,1024]{1,0:T(8,128)(2,1)S(1)}, bf16[128,1024]{1,0:T(8,128)(2,1)S(1)}, u32[]{:S(2)}, u32[]{:S(2)}) collective-permute-start(bf16[128,1024]{1,0:T(8,128)(2,1)S(1)} %get-tuple-element.33), channel_id=1, source_target_pairs={{0,64},{32,96},{64,128},{96,160},{128,192},{160,224},{192,0},{224,... | collective-permute-start | bytes 786440 | tf_op jit(solution)/shard_map/ppermute | solution.py:415
  54.3 14.8 %collective-permute-start.7 = (bf16[128,1024]{1,0:T(8,128)(2,1)S(1)}, bf16[128,1024]{1,0:T(8,128)(2,1)S(1)}, u32[]{:S(2)}, u32[]{:S(2)}) collective-permute-start(bf16[128,1024]{1,0:T(8,128)(2,1)S(1)} %get-tuple-element.31), channel_id=1, source_target_pairs={{0,192},{32,224},{64,0},{96,32},{128,64},{160,96},{192,128},{224,1... | collective-permute-start | bytes 786440 | tf_op jit(solution)/shard_map/ppermute | solution.py:415
  56.4 12.7 %collective-permute-start.8 = (bf16[272,1024]{1,0:T(8,128)(2,1)S(1)}, bf16[272,1024]{1,0:T(8,128)(2,1)S(1)}, u32[]{:S(2)}, u32[]{:S(2)}) collective-permute-start(bf16[272,1024]{1,0:T(8,128)(2,1)S(1)} %pad_maximum_fusion.1), channel_id=1, source_target_pairs={{0,32},{32,0},{64,96},{96,64},{128,160},{160,128},{192,224},{224,1... | collective-permute-start | bytes 1671176 | tf_op jit(solution)/shard_map/ppermute | solution.py:415
  72.2 4.3 %collective-permute-start.9 = (f32[32,128]{1,0:T(8,128)S(1)}, f32[32,128]{1,0:T(8,128)S(1)}, u32[]{:S(2)}, u32[]{:S(2)}) collective-permute-start(f32[32,128]{1,0:T(8,128)S(1)} %get-tuple-element.26), channel_id=1, source_target_pairs={{0,1},{1,0},{2,3},{3,2},{4,5},{5,4},{6,7},{7,6},{8,9},{9,8},{10,11... | collective-permute-start | bytes 49160 | tf_op jit(solution)/shard_map/ppermute | solution.py:390
  77.1 8.8 %all-to-all-start = ((f32[8,24,128]{2,1,0:T(8,128)}), f32[8,24,128]{2,1,0:T(8,128)S(1)}, u32[]{:S(2)}, u32[]{:S(2)}) async-start(f32[8,24,128]{2,1,0:T(8,128)} %broadcast_in_dim.27), calls=%async_computation | async-start | bytes 196608 | tf_op jit(solution)/shard_map/all_to_all | solution.py:391
  106.1 4.4 %copy-start.5 = (f32[32,128]{1,0:T(8,128)}, f32[32,128]{1,0:T(8,128)S(1)}, u32[]{:S(2)}) copy-start(f32[32,128]{1,0:T(8,128)S(1)} %reduce_sum.19.own_ref) | copy-start | bytes 49156
  106.1 4.4 %collective-permute-start.10 = (f32[32,128]{1,0:T(8,128)S(1)}, f32[32,128]{1,0:T(8,128)S(1)}, u32[]{:S(2)}, u32[]{:S(2)}) collective-permute-start(f32[32,128]{1,0:T(8,128)S(1)} %reduce_sum.19.own_ref), channel_id=1, source_target_pairs={{0,1},{1,0},{2,3},{3,2},{4,5},{5,4},{6,7},{7,6},{8,9},{9,8},{10,11... | collective-permute-start | bytes 49160 | tf_op jit(solution)/shard_map/ppermute | solution.py:394
  110.5 0.6 copy-start.6
where the time goes:
time: 115 us
  Pallas kernels  34.5 us (30%)
  starting transfers between devices  25.4 us (22%)
  waiting for transfers between devices  25.3 us (22%)
  blocking collectives  20.1 us (17%)
  local copies, waits for them, and re-layouts  7.75 us (7%)
    pallas_call x3, Pallas kernels, particle_terms(): pl.pallas_call(body, in_specs=specs, out_specs=[VMEM] * len(out_shape), o...  21.6 us
    all_to_all x1, blocking collectives, reduce_all(): lax.all_to_all(spread(mine, 16), 'pix', 0, 0, axis_index_groups=CORE_GROUPS)  20.1 us
    ppermute x9, waiting for transfers between devices, hop(): return lax.ppermute(block, 'dom', perm)  18.3 us
    ppermute x9, starting transfers between devices, hop(): return lax.ppermute(block, 'dom', perm)  15 us
    pallas_call x1, Pallas kernels, sort_particles(): pl.pallas_call(sort_kernel, grid=(cols // 512,), in_specs=[SMEM, SMEM, ro...  9.52 us
    unnamed x18, local copies, waits for them, and re-layouts  5.79 us
    all_to_all x1, waiting for transfers between devices, reduce_all(): moments = jnp.sum(lax.all_to_all(spread(mine[:24], 8), 'dom', 0, 0), axis=0)  5.38 us
    ppermute x1, starting transfers between devices, reduce_all(): other = lax.ppermute(mine, 'pix', CORE_SWAP)  3.57 us
  transfers between devices with their start and end apart: 12, of which 7 were waited for; matrix products, arithmetic and copies ran while one was open for 5% of the time, Pallas kernels for 25%

commit v1 on v0

--- a/solution.py
+++ b/solution.py
@@ -35,7 +35,7 @@
 
 
 def params():
-    return pltpu.CompilerParams(vmem_limit_bytes=28 * 1024 * 1024)
+    return pltpu.CompilerParams(vmem_limit_bytes=16 * 1024 * 1024)
 
 
 def horner(coeffs, z):
@@ -107,8 +107,8 @@
             SMEM,
         ],
         out_shape=[
-            jax.ShapeDtypeStruct((parts, cols), BF16),
-            jax.ShapeDtypeStruct((parts, parts), BF16),
+            pltpu.HBM((parts, cols), BF16),
+            pltpu.HBM((parts, parts), BF16),
             jax.ShapeDtypeStruct((parts, 16), F32),
             jax.ShapeDtypeStruct((16, parts), F32),
             jax.ShapeDtypeStruct((9,), jnp.int32),
@@ -146,7 +146,7 @@
 
 
 def row_range(stage, parts):
-    return [(0, 768, 256), (256, parts, 256), (768, parts, 128)][stage]
+    return [(0, 768, 256), (256, parts, 256), (832, parts, 192)][stage]
 
 
 def terms_kernel(stage, fill, refs):
@@ -162,7 +162,7 @@
     refs, work = refs[:-7], refs[-7:]
     table, image, sums, basis, pairs, table_sem, image_sem = work
     if late:
-        keep_ref, send_ref, moment_ref, grad_ref, full = refs[-5:]
+        keep_ref, send_ref, grad_ref, moment_ref, full = refs[-5:]
         pieces = refs[:-5]
     else:
         moment_ref, grad_ref, token_ref = refs[-3:]
@@ -272,17 +272,10 @@
     moment_ref[RIGHT_AT:, :] = right
 
     if late:
-        grads = grad_ref[...]
         moments = moment_ref[...]
-        packed = jnp.concatenate([moments[: MOMENTS // 2], moments[MOMENTS // 2 :]], axis=1)
-        for h in range(2):
-            full[32 * h : 32 * h + 24, :] = packed[24 * h : 24 * h + 24]
-            for r in range(4):
-                at = 512 * h + 128 * r
-                full[32 * h + 24 + r : 32 * h + 25 + r, :] = grads[0:1, at : at + 128]
-                full[32 * h + 28 + r : 32 * h + 29 + r, :] = grads[1:2, at : at + 128]
-        keep_ref[...] = full[pl.ds(pl.multiple_of(core[0] * 32, 32), 32), :]
-        send_ref[...] = full[pl.ds(pl.multiple_of((1 - core[0]) * 32, 32), 32), :]
+        full[...] = jnp.concatenate([moments[: MOMENTS // 2], moments[MOMENTS // 2 :]], axis=1)
+        keep_ref[...] = full[pl.ds(pl.multiple_of(core[0] * 24, 8), 24), :]
+        send_ref[...] = full[pl.ds(pl.multiple_of((1 - core[0]) * 24, 8), 24), :]
 
 
 def particle_terms(stage, fill, first, counts, mark_cols, mark_rows, images, pieces, before=(), core=None):
@@ -298,7 +291,7 @@
     specs += [pl.BlockSpec(memory_space=pltpu.HBM)] + [pl.BlockSpec(memory_space=pl.ANY)] * len(pieces)
     moments = jax.ShapeDtypeStruct((MOMENTS, GROUPS), F32)
     grads = jax.ShapeDtypeStruct((2, parts), F32)
-    half = jax.ShapeDtypeStruct((32, 128), F32)
+    half = jax.ShapeDtypeStruct((24, 128), F32)
     kb_from, kb_to = STAGES[stage]
     row_from, row_to, _ = row_range(stage, parts)
     work = [
@@ -311,12 +304,8 @@
         pltpu.SemaphoreType.DMA((1,)),
     ]
     if late:
-        out_shape = [half, half]
-        scratch = [
-            pltpu.VMEM(moments.shape, F32),
-            pltpu.VMEM(grads.shape, F32),
-            pltpu.VMEM((64, 128), F32),
-        ] + work
+        out_shape = [half, half, grads]
+        scratch = [pltpu.VMEM(moments.shape, F32), pltpu.VMEM((48, 128), F32)] + work
     else:
         out_shape = [moments, grads, jax.ShapeDtypeStruct((16, pix_count), BF16)]
         scratch = work
@@ -340,11 +329,53 @@
     )(*operands)
 
 
-def whiten_kernel(core, own_ref, other_ref, perm_ref, white_ref, score_ref, both, rows, perm, perm_sem, split):
+def unsort_kernel(core, grad_ref, perm_ref, keep_ref, send_ref, split, full, perm, perm_sem):
     perm_load = pltpu.make_async_copy(perm_ref, perm, perm_sem.at[0])
     perm_load.start()
-    both[pl.ds(pl.multiple_of(core[0] * 32, 32), 32), :] = own_ref[...]
-    both[pl.ds(pl.multiple_of((1 - core[0]) * 32, 32), 32), :] = other_ref[...]
+    rest = grad_ref[...]
+    split[...] = jnp.zeros_like(split)
+    for k in range(3):
+        term = rest.astype(BF16).astype(F32)
+        split[2 * k : 2 * k + 2, :] = term
+        rest = rest - term
+    perm_load.wait()
+    back = jnp.dot(split[...].astype(BF16), perm[...], preferred_element_type=F32)
+    grads = back[0:2] + back[2:4] + back[4:6]
+    for h in range(2):
+        for r in range(4):
+            at = 512 * h + 128 * r
+            full[8 * h + r : 8 * h + r + 1, :] = grads[0:1, at : at + 128]
+            full[8 * h + 4 + r : 8 * h + 5 + r, :] = grads[1:2, at : at + 128]
+    keep_ref[...] = full[pl.ds(pl.multiple_of(core[0] * 8, 8), 8), :]
+    send_ref[...] = full[pl.ds(pl.multiple_of((1 - core[0]) * 8, 8), 8), :]
+
+
+def unsort(core, grads, perm):
+    half = jax.ShapeDtypeStruct((8, 128), F32)
+    return pl.pallas_call(
+        unsort_kernel,
+        in_specs=[SMEM, VMEM, pl.BlockSpec(memory_space=pltpu.HBM)],
+        out_shape=[half, half],
+        scratch_shapes=[
+            pltpu.VMEM((16, perm.shape[0]), F32),
+            pltpu.VMEM((16, 128), F32),
+            pltpu.VMEM(perm.shape, BF16),
+            pltpu.SemaphoreType.DMA((1,)),
+        ],
+        compiler_params=params(),
+        name="unsort",
+    )(core, grads, perm)
+
+
+def whiten_kernel(core, own_ref, other_ref, white_ref, score_ref, both, rows, sem):
+    loads = [
+        pltpu.make_async_copy(ref, both.at[pl.ds(pl.multiple_of(at * 32, 32), 32), :], sem.at[i])
+        for i, (ref, at) in enumerate([(own_ref, core[0]), (other_ref, 1 - core[0])])
+    ]
+    for copy in loads:
+        copy.start()
+    for copy in loads:
+        copy.wait()
     low = jnp.concatenate([both[0:24, :], both[32:56, :]], axis=0)
     moments = jnp.concatenate([low[:, :GROUPS], low[:, GROUPS:]], axis=0)
     at = 0
@@ -365,49 +396,39 @@
         for i in range(j + 1, ZERN):
             line[i] = line[i] - col[i : i + 1] * col
     white_ref[...] = done[:ZERN]
-    split[...] = jnp.zeros_like(split)
     for h in range(2):
         grad = both[32 * h + 24 : 32 * h + 28, :]
         curv = both[32 * h + 28 : 32 * h + 32, :]
-        score = -grad * lax.rsqrt(curv + 1e-06)
-        for r in range(4):
-            at = 512 * h + 128 * r
-            rest = score[r : r + 1]
-            for k in range(3):
-                term = rest.astype(BF16).astype(F32)
-                split[k : k + 1, at : at + 128] = term
-                rest = rest - term
-    perm_load.wait()
-    back = jnp.dot(split[...].astype(BF16), perm[...], preferred_element_type=F32)
-    score_ref[...] = back[0:1] + back[1:2] + back[2:3]
+        score_ref[4 * h : 4 * h + 4, :] = -grad * lax.rsqrt(curv + 1e-06)
 
 
 def spread(block, count):
     return jnp.broadcast_to(block[None], (count,) + block.shape)
 
 
-def reduce_all(core, keep, send, perm):
+def reduce_all(core, keep, send, grads, perm):
     mine = keep + lax.ppermute(send, "pix", CORE_SWAP)
-    moments = jnp.sum(lax.all_to_all(spread(mine[:24], 8), "dom", 0, 0), axis=0)
-    mine = jnp.concatenate([moments, mine[24:]], axis=0)
+    moments = jnp.sum(lax.all_to_all(spread(mine, 8), "dom", 0, 0), axis=0)
+    keep, send = unsort(core, grads, perm)
+    grads = keep + lax.ppermute(send, "pix", CORE_SWAP)
+    mine = jnp.concatenate([moments, grads], axis=0)
     mine = jnp.sum(lax.all_to_all(spread(mine, 16), "pix", 0, 0, axis_index_groups=CORE_GROUPS), axis=0)
     other = lax.ppermute(mine, "pix", CORE_SWAP)
     white, score = pl.pallas_call(
         whiten_kernel,
-        in_specs=[SMEM, VMEM, VMEM, pl.BlockSpec(memory_space=pltpu.HBM)],
+        in_specs=[SMEM] + [pl.BlockSpec(memory_space=pl.ANY)] * 2,
         out_shape=[
             jax.ShapeDtypeStruct((ZERN, GROUPS), F32),
-            jax.ShapeDtypeStruct((1, perm.shape[0]), F32),
+            jax.ShapeDtypeStruct((8, 128), F32),
         ],
         scratch_shapes=[
             pltpu.VMEM((64, 128), F32),
             pltpu.VMEM((ZERN, 16, GROUPS), F32),
-            pltpu.VMEM(perm.shape, BF16),
-            pltpu.SemaphoreType.DMA((1,)),
-            pltpu.VMEM((16, perm.shape[0]), F32),
+            pltpu.SemaphoreType.DMA((2,)),
         ],
+        compiler_params=params(),
         name="whiten",
-    )(core, mine, other, perm)
+    )(core, mine, other)
     return white.T, score.reshape(-1)
 
 
@@ -426,7 +447,7 @@
     next_b = parted(2, 0, 0, 512, half)
     far = parted(0, 256, 512, 128, 0) + parted(1, 256, 640, 128, 0)
     far += parted(0, 384, 512, 128, half) + parted(1, 384, 640, 128, half)
-    last = parted(0, 0, 0, 128, 0) + parted(1, 0, 128, 128, 0) + parted(2, 0, 0, 256, half)
+    last = parted(0, 0, 0, 256, half) + parted(1, 0, 0, 128, 0) + parted(2, 0, 128, 128, 0)
     return [own, next_a + next_b + far, last]
 
 
@@ -476,8 +497,8 @@
     far_a_1 = hop(down[128:256], Y_DOWN)
     far_b = hop(rows(up[384:512], down[384:512], token), X_SWAP)
     *sums, _ = particle_terms(1, fill[1], *shared, [up, down, b_side], sums)
-    keep, send = particle_terms(2, fill[2], *shared, [far_a_0, far_a_1, far_b], sums, core)
-    return reduce_all(core, keep, send, perm)
+    keep, send, grads = particle_terms(2, fill[2], *shared, [far_b, far_a_0, far_a_1], sums, core)
+    return reduce_all(core, keep, send, grads, perm)
 
 
 def solution(mesh):

time: 115 us -> 111 us (0.965)
  Pallas kernels: 34.5 us -> 30.8 us
  starting transfers between devices: 25.4 us -> 27 us
  waiting for transfers between devices: 25.3 us -> 23.7 us
    all_to_all x1, waiting for transfers between devices: 5.38 us -> 3.25 us  [reduce_all(): moments = jnp.sum(lax.all_to_all(spread(mine, 8), 'dom', 0, 0), axis=0)]
    pallas_call x3, Pallas kernels: 21.6 us -> 19.6 us  [particle_terms(): pl.pallas_call(body, in_specs=specs, out_specs=[VMEM] * len(out_shape), o...]
    pallas_call x1 -> x2, Pallas kernels: 3.33 us -> 1.38 us  [the longest x1 0.8 us: reduce_all(): pl.pallas_call(whiten_kernel, in_specs=[SMEM] + [pl.BlockSpec(memory_spac...]
    all_to_all x1, starting transfers between devices: 3.38 us -> 4.58 us  [reduce_all(): moments = jnp.sum(lax.all_to_all(spread(mine, 8), 'dom', 0, 0), axis=0)]
    unnamed x18 -> x16, local copies, waits for them, and re-layouts: 5.79 us -> 5.2 us
  transfers between devices with their start and end apart: 12 -> 13, of which waited for: 7 -> 9; matrix products, arithmetic and copies ran while one was open for 5% -> 6% of each run, Pallas kernels for 25% -> 24%
where the time goes in v1:
time: 111 us; the launch traced here: 110 us
  Pallas kernels  30.8 us (28%)
  starting transfers between devices  27 us (24%)
  waiting for transfers between devices  23.7 us (21%)
  blocking collectives  19.5 us (18%)
  local copies, waits for them, and re-layouts  7.91 us (7%)
    pallas_call x3, Pallas kernels, particle_terms(): pl.pallas_call(body, in_specs=specs, out_specs=[VMEM] * len(out_shape), o...  19.6 us
    all_to_all x1, blocking collectives, reduce_all(): lax.all_to_all(spread(mine, 16), 'pix', 0, 0, axis_index_groups=CORE_GROUPS)  19.5 us
    ppermute x9, waiting for transfers between devices, hop(): return lax.ppermute(block, 'dom', perm)  17.9 us
    ppermute x9, starting transfers between devices, hop(): return lax.ppermute(block, 'dom', perm)  14.9 us
    pallas_call x1, Pallas kernels, sort_particles(): pl.pallas_call(sort_kernel, grid=(cols // 512,), in_specs=[SMEM, SMEM, ro...  9.86 us
    unnamed x16, local copies, waits for them, and re-layouts  5.2 us
    all_to_all x1, starting transfers between devices, reduce_all(): moments = jnp.sum(lax.all_to_all(spread(mine, 8), 'dom', 0, 0), axis=0)  4.58 us
    ppermute x1, starting transfers between devices, reduce_all(): other = lax.ppermute(mine, 'pix', CORE_SWAP)  3.63 us
  transfers between devices with their start and end apart: 13, of which 9 were waited for; matrix products, arithmetic and copies ran while one was open for 6% of the time, Pallas kernels for 24%

profile of v1, /device:TPU:1, one launch (start us, length us, event | category | flops | bytes accessed | tf_op | source)
XLA Modules:
  0.0 110.5 jit_solution(16333393841385551268)
XLA Ops:
  0.6 1.5 %copy.10 = bf16[32,8,2,1024]{3,1,2,0:T(8,128)(2,1)S(1)} copy(bf16[32,8,2,1024]{3,2,1,0:T(2,128)(2,1)} %bitcast.24) | data formatting | bytes 2097152
  2.1 2.2 %collective-permute-start.1 = (bf16[256,2048]{1,0:T(8,128)(2,1)S(1)}, bf16[256,2048]{1,0:T(8,128)(2,1)S(1)}, u32[]{:S(2)}, u32[]{:S(2)}) collective-permute-start(bf16[256,2048]{1,0:T(8,128)(2,1)S(1)} %bitcast.15), channel_id=1, source_target_pairs={{0,64},{32,96},{64,128},{96,160},{128,192},{160,224},{192,0},{224,... | collective-permute-start | bytes 3145736 | tf_op jit(solution)/shard_map/ppermute | solution.py:436
  4.3 1.2 %collective-permute-start = (bf16[256,2048]{1,0:T(8,128)(2,1)S(1)}, bf16[256,2048]{1,0:T(8,128)(2,1)}, u32[]{:S(2)}, u32[]{:S(2)}) collective-permute-start(bf16[256,2048]{1,0:T(8,128)(2,1)S(1)} %bitcast.16), channel_id=1, source_target_pairs={{0,32},{32,0},{64,96},{96,64},{128,160},{160,128},{192,224},{224,1... | collective-permute-start | bytes 3145736 | tf_op jit(solution)/shard_map/ppermute | solution.py:436
  5.6 1.5 %collective-permute-start.2 = (bf16[256,2048]{1,0:T(8,128)(2,1)S(1)}, bf16[256,2048]{1,0:T(8,128)(2,1)S(1)}, u32[]{:S(2)}, u32[]{:S(2)}) collective-permute-start(bf16[256,2048]{1,0:T(8,128)(2,1)S(1)} %bitcast.17), channel_id=1, source_target_pairs={{0,192},{32,224},{64,0},{96,32},{128,64},{160,96},{192,128},{224,1... | collective-permute-start | bytes 3145736 | tf_op jit(solution)/shard_map/ppermute | solution.py:436
  7.1 3.7 %copy.9 = bf16[128,8,2,1024]{3,1,2,0:T(8,128)(2,1)S(1)} copy(bf16[128,8,2,1024]{3,2,1,0:T(2,128)(2,1)} %bitcast.23) | data formatting | bytes 8388608
  10.9 9.9 %sort_particles.1 = (bf16[1024,2048]{1,0:T(8,128)(2,1)}, bf16[1024,1024]{1,0:T(8,128)(2,1)}, f32[1024,16]{1,0:T(8,128)S(1)}, f32[16,1024]{1,0:T(8,128)S(1)}, s32[9]{0:T(128)S(1)}) custom-call(s32[1]{0:T(128)} %bitcast.2.place, s32[8]{0:T(128)S(1)} %copy-done.5, s32[1,1024]{1,0:T(1,128)S(1)} %bitcast.20, s32[1,1024]{1,0:T(1,128)S(1)} %bitcast.21, ...), custom_call_target="tpu_custom_call" | custom-call | flops 4294967296 | bytes 8388608 | tf_op jit(solution)/shard_map/sort_particles/pallas_call | solution.py:98
  20.7 0.8 slice.81
  21.5 5.2 %collective-permute-done.1.refs_7_ = bf16[256,2048]{1,0:T(8,128)(2,1)S(1)} collective-permute-done((bf16[256,2048]{1,0:T(8,128)(2,1)S(1)}, bf16[256,2048]{1,0:T(8,128)(2,1)S(1)}, u32[]{:S(2)}, u32[]{:S(2)}) %collective-permute-start.1) | collective-permute-done | bytes 1048608 | tf_op jit(solution)/shard_map/ppermute | solution.py:436
  26.7 1.2 %collective-permute-done.refs_6_ = bf16[256,2048]{1,0:T(8,128)(2,1)} collective-permute-done((bf16[256,2048]{1,0:T(8,128)(2,1)S(1)}, bf16[256,2048]{1,0:T(8,128)(2,1)}, u32[]{:S(2)}, u32[]{:S(2)}) %collective-permute-start) | collective-permute-done | bytes 1048608 | tf_op jit(solution)/shard_map/ppermute | solution.py:436
  27.9 1.1 fusion.5
  29.1 1.6 %collective-permute-start.3 = (bf16[512,1024]{1,0:T(8,128)(2,1)S(1)}, bf16[512,1024]{1,0:T(8,128)(2,1)S(1)}, u32[]{:S(2)}, u32[]{:S(2)}) collective-permute-start(bf16[512,1024]{1,0:T(8,128)(2,1)S(1)} %maximum_maximum_fusion), channel_id=1, source_target_pairs={{0,64},{32,96},{64,128},{96,160},{128,192},{160,224},{192,0},{224,... | collective-permute-start | bytes 3145736 | tf_op jit(solution)/shard_map/ppermute | solution.py:436
  30.9 1.2 %collective-permute-start.4 = (bf16[528,1024]{1,0:T(8,128)(2,1)S(1)}, bf16[528,1024]{1,0:T(8,128)(2,1)S(1)}, u32[]{:S(2)}, u32[]{:S(2)}) collective-permute-start(bf16[528,1024]{1,0:T(8,128)(2,1)S(1)} %pad_maximum_fusion), channel_id=1, source_target_pairs={{0,192},{32,224},{64,0},{96,32},{128,64},{160,96},{192,128},{224,1... | collective-permute-start | bytes 3244040 | tf_op jit(solution)/shard_map/ppermute | solution.py:436
  32.3 1.9 %collective-permute-start.5 = (bf16[512,1024]{1,0:T(8,128)(2,1)S(1)}, bf16[512,1024]{1,0:T(8,128)(2,1)S(1)}, u32[]{:S(2)}, u32[]{:S(2)}) collective-permute-start(bf16[512,1024]{1,0:T(8,128)(2,1)S(1)} %maximum_maximum_fusion.1), channel_id=1, source_target_pairs={{0,32},{32,0},{64,96},{96,64},{128,160},{160,128},{192,224},{224,1... | collective-permute-start | bytes 3145736 | tf_op jit(solution)/shard_map/ppermute | solution.py:436
  34.2 8.4 %terms_0.1 = (f32[96,64]{1,0:T(8,128)S(1)}, f32[2,1024]{1,0:T(2,128)S(1)}, bf16[16,1024]{1,0:T(8,128)(2,1)S(1)}) custom-call(s32[1]{0:T(128)} %bitcast.1.refs_0_.refs_1_, s32[9]{0:T(128)S(1)} %get-tuple-element.19.refs_1_.refs_2_, f32[1024,16]{1,0:T(8,128)S(1)} %get-tuple-element.20.refs_2_.refs_3_, f32[16,1024]{1,0:T(8,128)S(1)} %get-tuple-element.21.refs_3_.refs_4_, ...), custom_call_target="tpu_custom_call" | custom-call | flops 17179869184 | bytes 8388608 | tf_op jit(solution)/shard_map/terms_0/pallas_call | solution.py:316
  42.6 10.3 %collective-permute-done.3.refs_7_ = bf16[512,1024]{1,0:T(8,128)(2,1)S(1)} collective-permute-done((bf16[512,1024]{1,0:T(8,128)(2,1)S(1)}, bf16[512,1024]{1,0:T(8,128)(2,1)S(1)}, u32[]{:S(2)}, u32[]{:S(2)}) %collective-permute-start.3) | collective-permute-done | bytes 1048608 | tf_op jit(solution)/shard_map/ppermute | solution.py:436
  52.9 0.7 collective-permute-start.7
  54.3 1.3 %collective-permute-start.6 = (bf16[272,1024]{1,0:T(8,128)(2,1)S(1)}, bf16[272,1024]{1,0:T(8,128)(2,1)S(1)}, u32[]{:S(2)}, u32[]{:S(2)}) collective-permute-start(bf16[272,1024]{1,0:T(8,128)(2,1)S(1)} %pad_maximum_fusion.1), channel_id=1, source_target_pairs={{0,32},{32,0},{64,96},{96,64},{128,160},{160,128},{192,224},{224,1... | collective-permute-start | bytes 1671176 | tf_op jit(solution)/shard_map/ppermute | solution.py:436
  55.6 3.2 %collective-permute-start.8 = (bf16[128,1024]{1,0:T(8,128)(2,1)S(1)}, bf16[128,1024]{1,0:T(8,128)(2,1)S(1)}, u32[]{:S(2)}, u32[]{:S(2)}) collective-permute-start(bf16[128,1024]{1,0:T(8,128)(2,1)S(1)} %get-tuple-element.36), channel_id=1, source_target_pairs={{0,192},{32,224},{64,0},{96,32},{128,64},{160,96},{192,128},{224,1... | collective-permute-start | bytes 786440 | tf_op jit(solution)/shard_map/ppermute | solution.py:436
  58.8 7.6 %terms_1.1 = (f32[96,64]{1,0:T(8,128)S(1)}, f32[2,1024]{1,0:T(2,128)S(1)}, bf16[16,1024]{1,0:T(8,128)(2,1)}) custom-call(s32[1]{0:T(128)} %bitcast.1.refs_0_.refs_1_, s32[9]{0:T(128)S(1)} %get-tuple-element.19.refs_1_.refs_2_, f32[1024,16]{1,0:T(8,128)S(1)} %get-tuple-element.20.refs_2_.refs_3_, f32[16,1024]{1,0:T(8,128)S(1)} %get-tuple-element.21.refs_3_.refs_4_, ...), custom_call_target="tpu_custom_call" | custom-call | flops 12884901888 | bytes 8388608 | tf_op jit(solution)/shard_map/terms_1/pallas_call | solution.py:316
  66.4 0.7 collective-permute-done.6.refs_8_
  67.1 3.6 %terms_2.1 = (f32[24,128]{1,0:T(8,128)S(1)}, f32[24,128]{1,0:T(8,128)S(1)}, f32[2,1024]{1,0:T(2,128)S(1)}) custom-call(s32[1]{0:T(128)} %bitcast.refs_0_.core, s32[1]{0:T(128)} %bitcast.1.refs_0_.refs_1_, s32[9]{0:T(128)S(1)} %get-tuple-element.19.refs_1_.refs_2_, f32[1024,16]{1,0:T(8,128)S(1)} %get-tuple-element.20.refs_2_.refs_3_, ...), custom_call_target="tpu_custom_call" | custom-call | flops 4294967296 | bytes 8388608 | tf_op jit(solution)/shard_map/terms_2/pallas_call | solution.py:316
  70.7 3.2 %collective-permute-start.9 = (f32[24,128]{1,0:T(8,128)S(1)}, f32[24,128]{1,0:T(8,128)S(1)}, u32[]{:S(2)}, u32[]{:S(2)}) collective-permute-start(f32[24,128]{1,0:T(8,128)S(1)} %get-tuple-element.29), channel_id=1, source_target_pairs={{0,1},{1,0},{2,3},{3,2},{4,5},{5,4},{6,7},{7,6},{8,9},{9,8},{10,11... | collective-permute-start | bytes 36872 | tf_op jit(solution)/shard_map/ppermute | solution.py:410
  74.0 0.8 collective-permute-done.9
  74.8 0.7 broadcast_in_dim.27
  75.5 4.6 %all-to-all-start = ((f32[8,24,128]{2,1,0:T(8,128)}), f32[8,24,128]{2,1,0:T(8,128)S(1)}, u32[]{:S(2)}, u32[]{:S(2)}) async-start(f32[8,24,128]{2,1,0:T(8,128)} %broadcast_in_dim.27), calls=%async_computation | async-start | bytes 196608 | tf_op jit(solution)/shard_map/all_to_all | solution.py:411
  80.6 0.7 collective-permute-start.10
  81.3 0.8 collective-permute-done.10
  82.2 3.3 %all-to-all-done = f32[8,24,128]{2,1,0:T(8,128)S(1)} async-done(((f32[8,24,128]{2,1,0:T(8,128)}), f32[8,24,128]{2,1,0:T(8,128)S(1)}, u32[]{:S(2)}, u32[]{:S(2)}) %all-to-all-start) | async-done | bytes 98336 | tf_op jit(solution)/shard_map/all_to_all | solution.py:411
  85.5 19.5 %all_to_all.10 = f32[16,32,128]{2,1,0:T(8,128)S(1)} all-to-all(f32[16,32,128]{2,1,0:T(8,128)S(1)} %broadcast_in_dim.28), channel_id=1, replica_groups={{0,2,4,6,8,10,12,14,16,18,20,22,24,26,28,30},{1,3,5,7,9,11,13,15,17,19,..., dimensions={0} | all-to-all | bytes 524288 | tf_op jit(solution)/shard_map/all_to_all | solution.py:415
  105.0 3.6 %collective-permute-start.11 = (f32[32,128]{1,0:T(8,128)S(1)}, f32[32,128]{1,0:T(8,128)S(1)}, u32[]{:S(2)}, u32[]{:S(2)}) collective-permute-start(f32[32,128]{1,0:T(8,128)S(1)} %reduce_sum.19.own_ref), channel_id=1, source_target_pairs={{0,1},{1,0},{2,3},{3,2},{4,5},{5,4},{6,7},{7,6},{8,9},{9,8},{10,11... | collective-permute-start | bytes 49160 | tf_op jit(solution)/shard_map/ppermute | solution.py:416
  108.6 0.8 collective-permute-done.11.other_ref
  109.5 0.8 whiten.1
  (37 shorter events, 1.9 us)
Async XLA Ops:
  0.6 6.5 %copy-start.6 = (bf16[1024]{0:T(1024)(128)(2,1)S(1)}, bf16[1024]{0:T(1024)(128)(2,1)}, u32[]{:S(2)}) copy-start(bf16[1024]{0:T(1024)(128)(2,1)} %param.12) | copy-start | bytes 6148
  2.1 24.5 %collective-permute-start.1 = (bf16[256,2048]{1,0:T(8,128)(2,1)S(1)}, bf16[256,2048]{1,0:T(8,128)(2,1)S(1)}, u32[]{:S(2)}, u32[]{:S(2)}) collective-permute-start(bf16[256,2048]{1,0:T(8,128)(2,1)S(1)} %bitcast.15), channel_id=1, source_target_pairs={{0,64},{32,96},{64,128},{96,160},{128,192},{160,224},{192,0},{224,... | collective-permute-start | bytes 3145736 | tf_op jit(solution)/shard_map/ppermute | solution.py:436
  4.3 23.5 %collective-permute-start = (bf16[256,2048]{1,0:T(8,128)(2,1)S(1)}, bf16[256,2048]{1,0:T(8,128)(2,1)}, u32[]{:S(2)}, u32[]{:S(2)}) collective-permute-start(bf16[256,2048]{1,0:T(8,128)(2,1)S(1)} %bitcast.16), channel_id=1, source_target_pairs={{0,32},{32,0},{64,96},{96,64},{128,160},{160,128},{192,224},{224,1... | collective-permute-start | bytes 3145736 | tf_op jit(solution)/shard_map/ppermute | solution.py:436
  5.6 25.2 %collective-permute-start.2 = (bf16[256,2048]{1,0:T(8,128)(2,1)S(1)}, bf16[256,2048]{1,0:T(8,128)(2,1)S(1)}, u32[]{:S(2)}, u32[]{:S(2)}) collective-permute-start(bf16[256,2048]{1,0:T(8,128)(2,1)S(1)} %bitcast.17), channel_id=1, source_target_pairs={{0,192},{32,224},{64,0},{96,32},{128,64},{160,96},{192,128},{224,1... | collective-permute-start | bytes 3145736 | tf_op jit(solution)/shard_map/ppermute | solution.py:436
  7.1 3.7 %copy-start.2 = (s32[1024,1]{0,1:T(1,128)S(1)}, s32[1024,1]{0,1:T(1,128)}, u32[]{:S(2)}) copy-start(s32[1024,1]{0,1:T(1,128)} %param.9) | copy-start | bytes 12292
  7.1 3.7 %copy-start.3 = (s32[1024]{0:T(1024)S(1)}, s32[1024]{0:T(1024)}, u32[]{:S(2)}) copy-start(s32[1024]{0:T(1024)} %param.10) | copy-start | bytes 12292
  7.1 3.7 %copy-start.4 = (s32[1024]{0:T(1024)S(1)}, s32[1024]{0:T(1024)}, u32[]{:S(2)}) copy-start(s32[1024]{0:T(1024)} %param.11) | copy-start | bytes 12292
  7.1 3.7 %copy-start.5 = (s32[8]{0:T(128)S(1)}, s32[8]{0:T(128)}, u32[]{:S(2)}) copy-start(s32[8]{0:T(128)} %slot_class.1) | copy-start | bytes 100
  29.1 23.8 %collective-permute-start.3 = (bf16[512,1024]{1,0:T(8,128)(2,1)S(1)}, bf16[512,1024]{1,0:T(8,128)(2,1)S(1)}, u32[]{:S(2)}, u32[]{:S(2)}) collective-permute-start(bf16[512,1024]{1,0:T(8,128)(2,1)S(1)} %maximum_maximum_fusion), channel_id=1, source_target_pairs={{0,64},{32,96},{64,128},{96,160},{128,192},{160,224},{192,0},{224,... | collective-permute-start | bytes 3145736 | tf_op jit(solution)/shard_map/ppermute | solution.py:436
  30.9 3.3 %copy-start.1 = (bf16[1024,2048]{1,0:T(8,128)(2,1)S(1)}, bf16[1024,2048]{1,0:T(8,128)(2,1)}, u32[]{:S(2)}) copy-start(bf16[1024,2048]{1,0:T(8,128)(2,1)} %get-tuple-element.22.refs_4_.refs_6_.refs_7_) | copy-start | bytes 12582916
  30.9 23.3 %collective-permute-start.4 = (bf16[528,1024]{1,0:T(8,128)(2,1)S(1)}, bf16[528,1024]{1,0:T(8,128)(2,1)S(1)}, u32[]{:S(2)}, u32[]{:S(2)}) collective-permute-start(bf16[528,1024]{1,0:T(8,128)(2,1)S(1)} %pad_maximum_fusion), channel_id=1, source_target_pairs={{0,192},{32,224},{64,0},{96,32},{128,64},{160,96},{192,128},{224,1... | collective-permute-start | bytes 3244040 | tf_op jit(solution)/shard_map/ppermute | solution.py:436
  32.3 26.5 %collective-permute-start.5 = (bf16[512,1024]{1,0:T(8,128)(2,1)S(1)}, bf16[512,1024]{1,0:T(8,128)(2,1)S(1)}, u32[]{:S(2)}, u32[]{:S(2)}) collective-permute-start(bf16[512,1024]{1,0:T(8,128)(2,1)S(1)} %maximum_maximum_fusion.1), channel_id=1, source_target_pairs={{0,32},{32,0},{64,96},{96,64},{128,160},{160,128},{192,224},{224,1... | collective-permute-start | bytes 3145736 | tf_op jit(solution)/shard_map/ppermute | solution.py:436
  52.9 13.5 %collective-permute-start.7 = (bf16[128,1024]{1,0:T(8,128)(2,1)S(1)}, bf16[128,1024]{1,0:T(8,128)(2,1)S(1)}, u32[]{:S(2)}, u32[]{:S(2)}) collective-permute-start(bf16[128,1024]{1,0:T(8,128)(2,1)S(1)} %get-tuple-element.38), channel_id=1, source_target_pairs={{0,64},{32,96},{64,128},{96,160},{128,192},{160,224},{192,0},{224,... | collective-permute-start | bytes 786440 | tf_op jit(solution)/shard_map/ppermute | solution.py:436
  54.3 12.9 %collective-permute-start.6 = (bf16[272,1024]{1,0:T(8,128)(2,1)S(1)}, bf16[272,1024]{1,0:T(8,128)(2,1)S(1)}, u32[]{:S(2)}, u32[]{:S(2)}) collective-permute-start(bf16[272,1024]{1,0:T(8,128)(2,1)S(1)} %pad_maximum_fusion.1), channel_id=1, source_target_pairs={{0,32},{32,0},{64,96},{96,64},{128,160},{160,128},{192,224},{224,1... | collective-permute-start | bytes 1671176 | tf_op jit(solution)/shard_map/ppermute | solution.py:436
  55.6 10.8 %collective-permute-start.8 = (bf16[128,1024]{1,0:T(8,128)(2,1)S(1)}, bf16[128,1024]{1,0:T(8,128)(2,1)S(1)}, u32[]{:S(2)}, u32[]{:S(2)}) collective-permute-start(bf16[128,1024]{1,0:T(8,128)(2,1)S(1)} %get-tuple-element.36), channel_id=1, source_target_pairs={{0,192},{32,224},{64,0},{96,32},{128,64},{160,96},{192,128},{224,1... | collective-permute-start | bytes 786440 | tf_op jit(solution)/shard_map/ppermute | solution.py:436
  67.1 12.9 %copy-start = (bf16[1024,1024]{1,0:T(8,128)(2,1)S(1)}, bf16[1024,1024]{1,0:T(8,128)(2,1)}, u32[]{:S(2)}) copy-start(bf16[1024,1024]{1,0:T(8,128)(2,1)} %get-tuple-element.31.perm_ref) | copy-start | bytes 6291460
  70.7 4.1 %collective-permute-start.9 = (f32[24,128]{1,0:T(8,128)S(1)}, f32[24,128]{1,0:T(8,128)S(1)}, u32[]{:S(2)}, u32[]{:S(2)}) collective-permute-start(f32[24,128]{1,0:T(8,128)S(1)} %get-tuple-element.29), channel_id=1, source_target_pairs={{0,1},{1,0},{2,3},{3,2},{4,5},{5,4},{6,7},{7,6},{8,9},{9,8},{10,11... | collective-permute-start | bytes 36872 | tf_op jit(solution)/shard_map/ppermute | solution.py:410
  75.5 10.0 %all-to-all-start = ((f32[8,24,128]{2,1,0:T(8,128)}), f32[8,24,128]{2,1,0:T(8,128)S(1)}, u32[]{:S(2)}, u32[]{:S(2)}) async-start(f32[8,24,128]{2,1,0:T(8,128)} %broadcast_in_dim.27), calls=%async_computation | async-start | bytes 196608 | tf_op jit(solution)/shard_map/all_to_all | solution.py:411
  80.6 1.5 %collective-permute-start.10 = (f32[8,128]{1,0:T(8,128)S(1)}, f32[8,128]{1,0:T(8,128)S(1)}, u32[]{:S(2)}, u32[]{:S(2)}) collective-permute-start(f32[8,128]{1,0:T(8,128)S(1)} %get-tuple-element.33), channel_id=1, source_target_pairs={{0,1},{1,0},{2,3},{3,2},{4,5},{5,4},{6,7},{7,6},{8,9},{9,8},{10,11... | collective-permute-start | bytes 12296 | tf_op jit(solution)/shard_map/ppermute | solution.py:413
  105.0 4.5 %collective-permute-start.11 = (f32[32,128]{1,0:T(8,128)S(1)}, f32[32,128]{1,0:T(8,128)S(1)}, u32[]{:S(2)}, u32[]{:S(2)}) collective-permute-start(f32[32,128]{1,0:T(8,128)S(1)} %reduce_sum.19.own_ref), channel_id=1, source_target_pairs={{0,1},{1,0},{2,3},{3,2},{4,5},{5,4},{6,7},{7,6},{8,9},{9,8},{10,11... | collective-permute-start | bytes 49160 | tf_op jit(solution)/shard_map/ppermute | solution.py:416

commit v2 on v1

--- a/solution.py
+++ b/solution.py
@@ -145,8 +145,8 @@
     return [re1, im1, r3 * re1, r3 * im1, r5 * re1, r5 * im1, re3, im3, ro * re3, ro * im3, re5, im5]
 
 
-def row_range(stage, parts):
-    return [(0, 768, 256), (256, parts, 256), (832, parts, 192)][stage]
+def tile_edges(stage, parts):
+    return [(0, 256, 512, 768), (256, 416, 672, 928, parts), (832, parts)][stage]
 
 
 def terms_kernel(stage, fill, refs):
@@ -171,7 +171,8 @@
     parts = col_ref.shape[0]
     pix_count = image_ref.shape[1] // 2
     kb_from, kb_to = STAGES[stage]
-    row_from, row_to, tile = row_range(stage, parts)
+    edges = tile_edges(stage, parts)
+    row_from, row_to = edges[0], edges[-1]
 
     loads = []
     for i, (piece, src, src_col, dst, dst_col, rows, width) in enumerate(fill):
@@ -255,9 +256,9 @@
 
     for copy in loads:
         copy.wait()
-    for at in range(row_from, row_to, tile):
-        some = (counts[kb_from] < at + tile) & (counts[kb_to] > at)
-        pl.when(some)(functools.partial(work_on, at, tile))
+    for at, end in zip(edges[:-1], edges[1:]):
+        some = (counts[kb_from] < end) & (counts[kb_to] > at)
+        pl.when(some)(functools.partial(work_on, at, end - at))
 
     normal = lax.dot_general(
         pairs[...], sums[:, :pix_count], NT, precision=lax.Precision.HIGHEST, preferred_element_type=F32
@@ -293,7 +294,8 @@
     grads = jax.ShapeDtypeStruct((2, parts), F32)
     half = jax.ShapeDtypeStruct((24, 128), F32)
     kb_from, kb_to = STAGES[stage]
-    row_from, row_to, _ = row_range(stage, parts)
+    edges = tile_edges(stage, parts)
+    row_from, row_to = edges[0], edges[-1]
     work = [
         pltpu.VMEM((256 * (kb_to - kb_from), 2 * pix_count), BF16),
         pltpu.VMEM((row_to - row_from, 2 * pix_count), BF16),

time: 111 us -> 111 us (level)
  no operation moved by 1% of the time
where the time goes in v2:
time: 111 us; the launch traced here: 110 us
  Pallas kernels  30.9 us (28%)
  starting transfers between devices  27 us (24%)
  waiting for transfers between devices  23.6 us (21%)
  blocking collectives  19.5 us (18%)
  local copies, waits for them, and re-layouts  7.91 us (7%)
    pallas_call x3, Pallas kernels, particle_terms(): pl.pallas_call(body, in_specs=specs, out_specs=[VMEM] * len(out_shape), o...  19.6 us
    all_to_all x1, blocking collectives, reduce_all(): lax.all_to_all(spread(mine, 16), 'pix', 0, 0, axis_index_groups=CORE_GROUPS)  19.5 us
    ppermute x9, waiting for transfers between devices, hop(): return lax.ppermute(block, 'dom', perm)  17.9 us
    ppermute x9, starting transfers between devices, hop(): return lax.ppermute(block, 'dom', perm)  14.9 us
    pallas_call x1, Pallas kernels, sort_particles(): pl.pallas_call(sort_kernel, grid=(cols // 512,), in_specs=[SMEM, SMEM, ro...  9.86 us
    unnamed x16, local copies, waits for them, and re-layouts  5.2 us
    all_to_all x1, starting transfers between devices, reduce_all(): moments = jnp.sum(lax.all_to_all(spread(mine, 8), 'dom', 0, 0), axis=0)  4.58 us
    ppermute x1, starting transfers between devices, reduce_all(): other = lax.ppermute(mine, 'pix', CORE_SWAP)  3.63 us
  transfers between devices with their start and end apart: 13, of which 9 were waited for; matrix products, arithmetic and copies ran while one was open for 6% of the time, Pallas kernels for 24%

profile of v2, /device:TPU:1, one launch (start us, length us, event | category | flops | bytes accessed | tf_op | source)
XLA Modules:
  0.0 110.5 jit_solution(18293501427999516061)
XLA Ops:
  0.6 1.5 %copy.10 = bf16[32,8,2,1024]{3,1,2,0:T(8,128)(2,1)S(1)} copy(bf16[32,8,2,1024]{3,2,1,0:T(2,128)(2,1)} %bitcast.24) | data formatting | bytes 2097152
  2.1 2.2 %collective-permute-start.1 = (bf16[256,2048]{1,0:T(8,128)(2,1)S(1)}, bf16[256,2048]{1,0:T(8,128)(2,1)S(1)}, u32[]{:S(2)}, u32[]{:S(2)}) collective-permute-start(bf16[256,2048]{1,0:T(8,128)(2,1)S(1)} %bitcast.15), channel_id=1, source_target_pairs={{0,64},{32,96},{64,128},{96,160},{128,192},{160,224},{192,0},{224,... | collective-permute-start | bytes 3145736 | tf_op jit(solution)/shard_map/ppermute | solution.py:438
  4.3 1.2 %collective-permute-start = (bf16[256,2048]{1,0:T(8,128)(2,1)S(1)}, bf16[256,2048]{1,0:T(8,128)(2,1)}, u32[]{:S(2)}, u32[]{:S(2)}) collective-permute-start(bf16[256,2048]{1,0:T(8,128)(2,1)S(1)} %bitcast.16), channel_id=1, source_target_pairs={{0,32},{32,0},{64,96},{96,64},{128,160},{160,128},{192,224},{224,1... | collective-permute-start | bytes 3145736 | tf_op jit(solution)/shard_map/ppermute | solution.py:438
  5.6 1.5 %collective-permute-start.2 = (bf16[256,2048]{1,0:T(8,128)(2,1)S(1)}, bf16[256,2048]{1,0:T(8,128)(2,1)S(1)}, u32[]{:S(2)}, u32[]{:S(2)}) collective-permute-start(bf16[256,2048]{1,0:T(8,128)(2,1)S(1)} %bitcast.17), channel_id=1, source_target_pairs={{0,192},{32,224},{64,0},{96,32},{128,64},{160,96},{192,128},{224,1... | collective-permute-start | bytes 3145736 | tf_op jit(solution)/shard_map/ppermute | solution.py:438
  7.1 3.7 %copy.9 = bf16[128,8,2,1024]{3,1,2,0:T(8,128)(2,1)S(1)} copy(bf16[128,8,2,1024]{3,2,1,0:T(2,128)(2,1)} %bitcast.23) | data formatting | bytes 8388608
  10.9 9.9 %sort_particles.1 = (bf16[1024,2048]{1,0:T(8,128)(2,1)}, bf16[1024,1024]{1,0:T(8,128)(2,1)}, f32[1024,16]{1,0:T(8,128)S(1)}, f32[16,1024]{1,0:T(8,128)S(1)}, s32[9]{0:T(128)S(1)}) custom-call(s32[1]{0:T(128)} %bitcast.2.place, s32[8]{0:T(128)S(1)} %copy-done.5, s32[1,1024]{1,0:T(1,128)S(1)} %bitcast.20, s32[1,1024]{1,0:T(1,128)S(1)} %bitcast.21, ...), custom_call_target="tpu_custom_call" | custom-call | flops 4294967296 | bytes 8388608 | tf_op jit(solution)/shard_map/sort_particles/pallas_call | solution.py:98
  20.7 0.8 slice.81
  21.5 5.2 %collective-permute-done.1.refs_7_ = bf16[256,2048]{1,0:T(8,128)(2,1)S(1)} collective-permute-done((bf16[256,2048]{1,0:T(8,128)(2,1)S(1)}, bf16[256,2048]{1,0:T(8,128)(2,1)S(1)}, u32[]{:S(2)}, u32[]{:S(2)}) %collective-permute-start.1) | collective-permute-done | bytes 1048608 | tf_op jit(solution)/shard_map/ppermute | solution.py:438
  26.7 1.2 %collective-permute-done.refs_6_ = bf16[256,2048]{1,0:T(8,128)(2,1)} collective-permute-done((bf16[256,2048]{1,0:T(8,128)(2,1)S(1)}, bf16[256,2048]{1,0:T(8,128)(2,1)}, u32[]{:S(2)}, u32[]{:S(2)}) %collective-permute-start) | collective-permute-done | bytes 1048608 | tf_op jit(solution)/shard_map/ppermute | solution.py:438
  27.9 1.1 fusion.5
  29.1 1.6 %collective-permute-start.3 = (bf16[512,1024]{1,0:T(8,128)(2,1)S(1)}, bf16[512,1024]{1,0:T(8,128)(2,1)S(1)}, u32[]{:S(2)}, u32[]{:S(2)}) collective-permute-start(bf16[512,1024]{1,0:T(8,128)(2,1)S(1)} %maximum_maximum_fusion), channel_id=1, source_target_pairs={{0,64},{32,96},{64,128},{96,160},{128,192},{160,224},{192,0},{224,... | collective-permute-start | bytes 3145736 | tf_op jit(solution)/shard_map/ppermute | solution.py:438
  30.9 1.2 %collective-permute-start.4 = (bf16[528,1024]{1,0:T(8,128)(2,1)S(1)}, bf16[528,1024]{1,0:T(8,128)(2,1)S(1)}, u32[]{:S(2)}, u32[]{:S(2)}) collective-permute-start(bf16[528,1024]{1,0:T(8,128)(2,1)S(1)} %pad_maximum_fusion), channel_id=1, source_target_pairs={{0,192},{32,224},{64,0},{96,32},{128,64},{160,96},{192,128},{224,1... | collective-permute-start | bytes 3244040 | tf_op jit(solution)/shard_map/ppermute | solution.py:438
  32.3 1.9 %collective-permute-start.5 = (bf16[512,1024]{1,0:T(8,128)(2,1)S(1)}, bf16[512,1024]{1,0:T(8,128)(2,1)S(1)}, u32[]{:S(2)}, u32[]{:S(2)}) collective-permute-start(bf16[512,1024]{1,0:T(8,128)(2,1)S(1)} %maximum_maximum_fusion.1), channel_id=1, source_target_pairs={{0,32},{32,0},{64,96},{96,64},{128,160},{160,128},{192,224},{224,1... | collective-permute-start | bytes 3145736 | tf_op jit(solution)/shard_map/ppermute | solution.py:438
  34.2 8.4 %terms_0.1 = (f32[96,64]{1,0:T(8,128)S(1)}, f32[2,1024]{1,0:T(2,128)S(1)}, bf16[16,1024]{1,0:T(8,128)(2,1)S(1)}) custom-call(s32[1]{0:T(128)} %bitcast.1.refs_0_.refs_1_, s32[9]{0:T(128)S(1)} %get-tuple-element.19.refs_1_.refs_2_, f32[1024,16]{1,0:T(8,128)S(1)} %get-tuple-element.20.refs_2_.refs_3_, f32[16,1024]{1,0:T(8,128)S(1)} %get-tuple-element.21.refs_3_.refs_4_, ...), custom_call_target="tpu_custom_call" | custom-call | flops 17179869184 | bytes 8388608 | tf_op jit(solution)/shard_map/terms_0/pallas_call | solution.py:318
  42.6 10.3 %collective-permute-done.3.refs_7_ = bf16[512,1024]{1,0:T(8,128)(2,1)S(1)} collective-permute-done((bf16[512,1024]{1,0:T(8,128)(2,1)S(1)}, bf16[512,1024]{1,0:T(8,128)(2,1)S(1)}, u32[]{:S(2)}, u32[]{:S(2)}) %collective-permute-start.3) | collective-permute-done | bytes 1048608 | tf_op jit(solution)/shard_map/ppermute | solution.py:438
  52.9 0.7 collective-permute-start.7
  54.3 1.3 %collective-permute-start.6 = (bf16[272,1024]{1,0:T(8,128)(2,1)S(1)}, bf16[272,1024]{1,0:T(8,128)(2,1)S(1)}, u32[]{:S(2)}, u32[]{:S(2)}) collective-permute-start(bf16[272,1024]{1,0:T(8,128)(2,1)S(1)} %pad_maximum_fusion.1), channel_id=1, source_target_pairs={{0,32},{32,0},{64,96},{96,64},{128,160},{160,128},{192,224},{224,1... | collective-permute-start | bytes 1671176 | tf_op jit(solution)/shard_map/ppermute | solution.py:438
  55.6 3.2 %collective-permute-start.8 = (bf16[128,1024]{1,0:T(8,128)(2,1)S(1)}, bf16[128,1024]{1,0:T(8,128)(2,1)S(1)}, u32[]{:S(2)}, u32[]{:S(2)}) collective-permute-start(bf16[128,1024]{1,0:T(8,128)(2,1)S(1)} %get-tuple-element.36), channel_id=1, source_target_pairs={{0,192},{32,224},{64,0},{96,32},{128,64},{160,96},{192,128},{224,1... | collective-permute-start | bytes 786440 | tf_op jit(solution)/shard_map/ppermute | solution.py:438
  58.8 7.6 %terms_1.1 = (f32[96,64]{1,0:T(8,128)S(1)}, f32[2,1024]{1,0:T(2,128)S(1)}, bf16[16,1024]{1,0:T(8,128)(2,1)}) custom-call(s32[1]{0:T(128)} %bitcast.1.refs_0_.refs_1_, s32[9]{0:T(128)S(1)} %get-tuple-element.19.refs_1_.refs_2_, f32[1024,16]{1,0:T(8,128)S(1)} %get-tuple-element.20.refs_2_.refs_3_, f32[16,1024]{1,0:T(8,128)S(1)} %get-tuple-element.21.refs_3_.refs_4_, ...), custom_call_target="tpu_custom_call" | custom-call | flops 12884901888 | bytes 8388608 | tf_op jit(solution)/shard_map/terms_1/pallas_call | solution.py:318
  66.5 0.7 collective-permute-done.6.refs_8_
  67.1 3.6 %terms_2.1 = (f32[24,128]{1,0:T(8,128)S(1)}, f32[24,128]{1,0:T(8,128)S(1)}, f32[2,1024]{1,0:T(2,128)S(1)}) custom-call(s32[1]{0:T(128)} %bitcast.refs_0_.core, s32[1]{0:T(128)} %bitcast.1.refs_0_.refs_1_, s32[9]{0:T(128)S(1)} %get-tuple-element.19.refs_1_.refs_2_, f32[1024,16]{1,0:T(8,128)S(1)} %get-tuple-element.20.refs_2_.refs_3_, ...), custom_call_target="tpu_custom_call" | custom-call | flops 4294967296 | bytes 8388608 | tf_op jit(solution)/shard_map/terms_2/pallas_call | solution.py:318
  70.7 3.2 %collective-permute-start.9 = (f32[24,128]{1,0:T(8,128)S(1)}, f32[24,128]{1,0:T(8,128)S(1)}, u32[]{:S(2)}, u32[]{:S(2)}) collective-permute-start(f32[24,128]{1,0:T(8,128)S(1)} %get-tuple-element.29), channel_id=1, source_target_pairs={{0,1},{1,0},{2,3},{3,2},{4,5},{5,4},{6,7},{7,6},{8,9},{9,8},{10,11... | collective-permute-start | bytes 36872 | tf_op jit(solution)/shard_map/ppermute | solution.py:412
  74.0 0.8 collective-permute-done.9
  74.8 0.7 broadcast_in_dim.27
  75.5 4.6 %all-to-all-start = ((f32[8,24,128]{2,1,0:T(8,128)}), f32[8,24,128]{2,1,0:T(8,128)S(1)}, u32[]{:S(2)}, u32[]{:S(2)}) async-start(f32[8,24,128]{2,1,0:T(8,128)} %broadcast_in_dim.27), calls=%async_computation | async-start | bytes 196608 | tf_op jit(solution)/shard_map/all_to_all | solution.py:413
  80.6 0.7 collective-permute-start.10
  81.3 0.8 collective-permute-done.10
  82.2 3.3 %all-to-all-done = f32[8,24,128]{2,1,0:T(8,128)S(1)} async-done(((f32[8,24,128]{2,1,0:T(8,128)}), f32[8,24,128]{2,1,0:T(8,128)S(1)}, u32[]{:S(2)}, u32[]{:S(2)}) %all-to-all-start) | async-done | bytes 98336 | tf_op jit(solution)/shard_map/all_to_all | solution.py:413
  85.5 19.5 %all_to_all.10 = f32[16,32,128]{2,1,0:T(8,128)S(1)} all-to-all(f32[16,32,128]{2,1,0:T(8,128)S(1)} %broadcast_in_dim.28), channel_id=1, replica_groups={{0,2,4,6,8,10,12,14,16,18,20,22,24,26,28,30},{1,3,5,7,9,11,13,15,17,19,..., dimensions={0} | all-to-all | bytes 524288 | tf_op jit(solution)/shard_map/all_to_all | solution.py:417
  105.0 3.6 %collective-permute-start.11 = (f32[32,128]{1,0:T(8,128)S(1)}, f32[32,128]{1,0:T(8,128)S(1)}, u32[]{:S(2)}, u32[]{:S(2)}) collective-permute-start(f32[32,128]{1,0:T(8,128)S(1)} %reduce_sum.19.own_ref), channel_id=1, source_target_pairs={{0,1},{1,0},{2,3},{3,2},{4,5},{5,4},{6,7},{7,6},{8,9},{9,8},{10,11... | collective-permute-start | bytes 49160 | tf_op jit(solution)/shard_map/ppermute | solution.py:418
  108.6 0.8 collective-permute-done.11.other_ref
  109.5 0.8 whiten.1
  (37 shorter events, 1.9 us)
Async XLA Ops:
  0.6 6.5 %copy-start.6 = (bf16[1024]{0:T(1024)(128)(2,1)S(1)}, bf16[1024]{0:T(1024)(128)(2,1)}, u32[]{:S(2)}) copy-start(bf16[1024]{0:T(1024)(128)(2,1)} %param.12) | copy-start | bytes 6148
  2.1 24.5 %collective-permute-start.1 = (bf16[256,2048]{1,0:T(8,128)(2,1)S(1)}, bf16[256,2048]{1,0:T(8,128)(2,1)S(1)}, u32[]{:S(2)}, u32[]{:S(2)}) collective-permute-start(bf16[256,2048]{1,0:T(8,128)(2,1)S(1)} %bitcast.15), channel_id=1, source_target_pairs={{0,64},{32,96},{64,128},{96,160},{128,192},{160,224},{192,0},{224,... | collective-permute-start | bytes 3145736 | tf_op jit(solution)/shard_map/ppermute | solution.py:438
  4.3 23.5 %collective-permute-start = (bf16[256,2048]{1,0:T(8,128)(2,1)S(1)}, bf16[256,2048]{1,0:T(8,128)(2,1)}, u32[]{:S(2)}, u32[]{:S(2)}) collective-permute-start(bf16[256,2048]{1,0:T(8,128)(2,1)S(1)} %bitcast.16), channel_id=1, source_target_pairs={{0,32},{32,0},{64,96},{96,64},{128,160},{160,128},{192,224},{224,1... | collective-permute-start | bytes 3145736 | tf_op jit(solution)/shard_map/ppermute | solution.py:438
  5.6 25.2 %collective-permute-start.2 = (bf16[256,2048]{1,0:T(8,128)(2,1)S(1)}, bf16[256,2048]{1,0:T(8,128)(2,1)S(1)}, u32[]{:S(2)}, u32[]{:S(2)}) collective-permute-start(bf16[256,2048]{1,0:T(8,128)(2,1)S(1)} %bitcast.17), channel_id=1, source_target_pairs={{0,192},{32,224},{64,0},{96,32},{128,64},{160,96},{192,128},{224,1... | collective-permute-start | bytes 3145736 | tf_op jit(solution)/shard_map/ppermute | solution.py:438
  7.1 3.7 %copy-start.2 = (s32[1024,1]{0,1:T(1,128)S(1)}, s32[1024,1]{0,1:T(1,128)}, u32[]{:S(2)}) copy-start(s32[1024,1]{0,1:T(1,128)} %param.9) | copy-start | bytes 12292
  7.1 3.7 %copy-start.3 = (s32[1024]{0:T(1024)S(1)}, s32[1024]{0:T(1024)}, u32[]{:S(2)}) copy-start(s32[1024]{0:T(1024)} %param.10) | copy-start | bytes 12292
  7.1 3.7 %copy-start.4 = (s32[1024]{0:T(1024)S(1)}, s32[1024]{0:T(1024)}, u32[]{:S(2)}) copy-start(s32[1024]{0:T(1024)} %param.11) | copy-start | bytes 12292
  7.1 3.7 %copy-start.5 = (s32[8]{0:T(128)S(1)}, s32[8]{0:T(128)}, u32[]{:S(2)}) copy-start(s32[8]{0:T(128)} %slot_class.1) | copy-start | bytes 100
  29.1 23.8 %collective-permute-start.3 = (bf16[512,1024]{1,0:T(8,128)(2,1)S(1)}, bf16[512,1024]{1,0:T(8,128)(2,1)S(1)}, u32[]{:S(2)}, u32[]{:S(2)}) collective-permute-start(bf16[512,1024]{1,0:T(8,128)(2,1)S(1)} %maximum_maximum_fusion), channel_id=1, source_target_pairs={{0,64},{32,96},{64,128},{96,160},{128,192},{160,224},{192,0},{224,... | collective-permute-start | bytes 3145736 | tf_op jit(solution)/shard_map/ppermute | solution.py:438
  30.9 3.3 %copy-start.1 = (bf16[1024,2048]{1,0:T(8,128)(2,1)S(1)}, bf16[1024,2048]{1,0:T(8,128)(2,1)}, u32[]{:S(2)}) copy-start(bf16[1024,2048]{1,0:T(8,128)(2,1)} %get-tuple-element.22.refs_4_.refs_6_.refs_7_) | copy-start | bytes 12582916
  30.9 23.3 %collective-permute-start.4 = (bf16[528,1024]{1,0:T(8,128)(2,1)S(1)}, bf16[528,1024]{1,0:T(8,128)(2,1)S(1)}, u32[]{:S(2)}, u32[]{:S(2)}) collective-permute-start(bf16[528,1024]{1,0:T(8,128)(2,1)S(1)} %pad_maximum_fusion), channel_id=1, source_target_pairs={{0,192},{32,224},{64,0},{96,32},{128,64},{160,96},{192,128},{224,1... | collective-permute-start | bytes 3244040 | tf_op jit(solution)/shard_map/ppermute | solution.py:438
  32.3 26.5 %collective-permute-start.5 = (bf16[512,1024]{1,0:T(8,128)(2,1)S(1)}, bf16[512,1024]{1,0:T(8,128)(2,1)S(1)}, u32[]{:S(2)}, u32[]{:S(2)}) collective-permute-start(bf16[512,1024]{1,0:T(8,128)(2,1)S(1)} %maximum_maximum_fusion.1), channel_id=1, source_target_pairs={{0,32},{32,0},{64,96},{96,64},{128,160},{160,128},{192,224},{224,1... | collective-permute-start | bytes 3145736 | tf_op jit(solution)/shard_map/ppermute | solution.py:438
  52.9 13.5 %collective-permute-start.7 = (bf16[128,1024]{1,0:T(8,128)(2,1)S(1)}, bf16[128,1024]{1,0:T(8,128)(2,1)S(1)}, u32[]{:S(2)}, u32[]{:S(2)}) collective-permute-start(bf16[128,1024]{1,0:T(8,128)(2,1)S(1)} %get-tuple-element.38), channel_id=1, source_target_pairs={{0,64},{32,96},{64,128},{96,160},{128,192},{160,224},{192,0},{224,... | collective-permute-start | bytes 786440 | tf_op jit(solution)/shard_map/ppermute | solution.py:438
  54.3 12.9 %collective-permute-start.6 = (bf16[272,1024]{1,0:T(8,128)(2,1)S(1)}, bf16[272,1024]{1,0:T(8,128)(2,1)S(1)}, u32[]{:S(2)}, u32[]{:S(2)}) collective-permute-start(bf16[272,1024]{1,0:T(8,128)(2,1)S(1)} %pad_maximum_fusion.1), channel_id=1, source_target_pairs={{0,32},{32,0},{64,96},{96,64},{128,160},{160,128},{192,224},{224,1... | collective-permute-start | bytes 1671176 | tf_op jit(solution)/shard_map/ppermute | solution.py:438
  55.6 10.9 %collective-permute-start.8 = (bf16[128,1024]{1,0:T(8,128)(2,1)S(1)}, bf16[128,1024]{1,0:T(8,128)(2,1)S(1)}, u32[]{:S(2)}, u32[]{:S(2)}) collective-permute-start(bf16[128,1024]{1,0:T(8,128)(2,1)S(1)} %get-tuple-element.36), channel_id=1, source_target_pairs={{0,192},{32,224},{64,0},{96,32},{128,64},{160,96},{192,128},{224,1... | collective-permute-start | bytes 786440 | tf_op jit(solution)/shard_map/ppermute | solution.py:438
  67.1 12.9 %copy-start = (bf16[1024,1024]{1,0:T(8,128)(2,1)S(1)}, bf16[1024,1024]{1,0:T(8,128)(2,1)}, u32[]{:S(2)}) copy-start(bf16[1024,1024]{1,0:T(8,128)(2,1)} %get-tuple-element.31.perm_ref) | copy-start | bytes 6291460
  70.7 4.1 %collective-permute-start.9 = (f32[24,128]{1,0:T(8,128)S(1)}, f32[24,128]{1,0:T(8,128)S(1)}, u32[]{:S(2)}, u32[]{:S(2)}) collective-permute-start(f32[24,128]{1,0:T(8,128)S(1)} %get-tuple-element.29), channel_id=1, source_target_pairs={{0,1},{1,0},{2,3},{3,2},{4,5},{5,4},{6,7},{7,6},{8,9},{9,8},{10,11... | collective-permute-start | bytes 36872 | tf_op jit(solution)/shard_map/ppermute | solution.py:412
  75.5 10.0 %all-to-all-start = ((f32[8,24,128]{2,1,0:T(8,128)}), f32[8,24,128]{2,1,0:T(8,128)S(1)}, u32[]{:S(2)}, u32[]{:S(2)}) async-start(f32[8,24,128]{2,1,0:T(8,128)} %broadcast_in_dim.27), calls=%async_computation | async-start | bytes 196608 | tf_op jit(solution)/shard_map/all_to_all | solution.py:413
  80.6 1.5 %collective-permute-start.10 = (f32[8,128]{1,0:T(8,128)S(1)}, f32[8,128]{1,0:T(8,128)S(1)}, u32[]{:S(2)}, u32[]{:S(2)}) collective-permute-start(f32[8,128]{1,0:T(8,128)S(1)} %get-tuple-element.33), channel_id=1, source_target_pairs={{0,1},{1,0},{2,3},{3,2},{4,5},{5,4},{6,7},{7,6},{8,9},{9,8},{10,11... | collective-permute-start | bytes 12296 | tf_op jit(solution)/shard_map/ppermute | solution.py:415
  105.0 4.5 %collective-permute-start.11 = (f32[32,128]{1,0:T(8,128)S(1)}, f32[32,128]{1,0:T(8,128)S(1)}, u32[]{:S(2)}, u32[]{:S(2)}) collective-permute-start(f32[32,128]{1,0:T(8,128)S(1)} %reduce_sum.19.own_ref), channel_id=1, source_target_pairs={{0,1},{1,0},{2,3},{3,2},{4,5},{5,4},{6,7},{7,6},{8,9},{9,8},{10,11... | collective-permute-start | bytes 49160 | tf_op jit(solution)/shard_map/ppermute | solution.py:418

commit v3 on v2

--- a/solution.py
+++ b/solution.py
@@ -3,6 +3,7 @@
 
 import jax
 import jax.numpy as jnp
+import numpy as np
 from jax import lax
 from jax.experimental import pallas as pl
 from jax.experimental.pallas import tpu as pltpu
@@ -16,8 +17,8 @@
 RIDGE = 1.0
 
 WIDE = 256
-MOMENTS = 96
-RIGHT_AT = 80
+MOMENTS = 48
+RIGHT_AT = 36
 
 SIN_POLY = (3.141592580044675, -5.167706878922935, 2.5500313772212047, -0.5980451737557255, 0.07722012821305138)
 COS_POLY = (0.9999999534415752, -4.934792857330457, 4.058411894717311, -1.3318800570964462, 0.2196966127309024)
@@ -122,6 +123,42 @@
     )(place, slot_class, class_row, pose_row, group_row, defocus_row, images)
 
 
+def legendre(q, count):
+    x = 2.0 * q - 1.0
+    rows = [q * 0.0 + 1.0, x]
+    for n in range(1, count - 1):
+        rows.append(((2 * n + 1) * x * rows[n] - n * rows[n - 1]) / (n + 1))
+    return rows[:count]
+
+
+def product_rows(freq_x, freq_y):
+    q = freq_x * freq_x + freq_y * freq_y
+    polys = legendre(q, 5)
+    rows = [q * p for p in polys]
+    re2, im2 = freq_x * freq_x - freq_y * freq_y, 2.0 * freq_x * freq_y
+    re, im = re2, im2
+    for count in (5, 4, 3, 2, 1):
+        for p in polys[:count]:
+            rows += [re * p, im * p]
+        re, im = re * re2 - im * im2, re * im2 + im * re2
+    return rows
+
+
+def product_weights():
+    angle = np.arange(24) * (2.0 * np.pi / 24) + 0.1
+    radius = np.sqrt((np.cos((np.arange(8) + 0.5) * (np.pi / 8)) + 1.0) / 2.0)
+    x = (radius[:, None] * np.cos(angle)).reshape(-1)
+    y = (radius[:, None] * np.sin(angle)).reshape(-1)
+    zern = zernike_rows(x, y)
+    pairs = np.stack([zern[j] * zern[k] for j in range(ZERN) for k in range(j, ZERN)], axis=1)
+    rows = np.stack(product_rows(x, y), axis=1)
+    weights = np.linalg.lstsq(rows, pairs, rcond=None)[0].T
+    weights = np.where(np.abs(weights) < 1e-10, 0.0, np.round(weights, 12))
+    out = np.zeros((80, RIGHT_AT + 4))
+    out[:PAIRS, : rows.shape[1]] = weights
+    return out.astype(np.float32)
+
+
 def pixel_grid(first, count):
     index = first + lax.broadcasted_iota(jnp.int32, (1, count), 1)
     scale = math.sqrt(2.0) / BOX
@@ -160,7 +197,7 @@
         refs = refs[2:]
     image_ref = refs.pop(0)
     refs, work = refs[:-7], refs[-7:]
-    table, image, sums, basis, pairs, table_sem, image_sem = work
+    table, image, sums, basis, products, table_sem, image_sem = work
     if late:
         keep_ref, send_ref, grad_ref, moment_ref, full = refs[-5:]
         pieces = refs[:-5]
@@ -245,14 +282,12 @@
         grad_ref[0:1, here] += jnp.sum(grad_sum.T, axis=0, keepdims=True)
         grad_ref[1:2, here] += jnp.sum(curv_sum.T, axis=0, keepdims=True)
 
+    products[...] = jnp.zeros_like(products)
+    for j, row in enumerate(product_rows(freq_x, freq_y)):
+        products[j : j + 1, :] = row
     basis[...] = jnp.zeros_like(basis)
     for j, row in enumerate(zernike_rows(freq_x, freq_y)):
         basis[j : j + 1, :] = row
-    pairs[72:80, :] = jnp.zeros((8, pix_count), F32)
-    at = 0
-    for j in range(ZERN):
-        pairs[at : at + ZERN - j, :] = basis[j : j + 1, :] * basis[j:ZERN, :]
-        at += ZERN - j
 
     for copy in loads:
         copy.wait()
@@ -261,22 +296,24 @@
         pl.when(some)(functools.partial(work_on, at, end - at))
 
     normal = lax.dot_general(
-        pairs[...], sums[:, :pix_count], NT, precision=lax.Precision.HIGHEST, preferred_element_type=F32
+        products[...], sums[:, :pix_count], NT, precision=lax.Precision.HIGHEST, preferred_element_type=F32
     )
     right = lax.dot_general(
         basis[...], sums[:, pix_count:], NT, precision=lax.Precision.HIGHEST, preferred_element_type=F32
     )
+    moments = jnp.concatenate([normal[:RIGHT_AT], right[:ZERN]], axis=0)
     if stage > 0:
-        normal = normal + old_moments[0:RIGHT_AT, :]
-        right = right + old_moments[RIGHT_AT:, :]
-    moment_ref[0:RIGHT_AT, :] = normal
-    moment_ref[RIGHT_AT:, :] = right
+        moments = moments + old_moments[...]
+    moment_ref[...] = moments
 
     if late:
-        moments = moment_ref[...]
-        full[...] = jnp.concatenate([moments[: MOMENTS // 2], moments[MOMENTS // 2 :]], axis=1)
-        keep_ref[...] = full[pl.ds(pl.multiple_of(core[0] * 24, 8), 24), :]
-        send_ref[...] = full[pl.ds(pl.multiple_of((1 - core[0]) * 24, 8), 24), :]
+        half = MOMENTS // 2
+        full[...] = jnp.zeros_like(full)
+        packed = jnp.concatenate([moments[:half], moments[half:]], axis=1)
+        full[0:12] = packed[0:12]
+        full[16:28] = packed[12:24]
+        keep_ref[...] = full[pl.ds(pl.multiple_of(core[0] * 16, 16), 16), :]
+        send_ref[...] = full[pl.ds(pl.multiple_of((1 - core[0]) * 16, 16), 16), :]
 
 
 def particle_terms(stage, fill, first, counts, mark_cols, mark_rows, images, pieces, before=(), core=None):
@@ -292,7 +329,7 @@
     specs += [pl.BlockSpec(memory_space=pltpu.HBM)] + [pl.BlockSpec(memory_space=pl.ANY)] * len(pieces)
     moments = jax.ShapeDtypeStruct((MOMENTS, GROUPS), F32)
     grads = jax.ShapeDtypeStruct((2, parts), F32)
-    half = jax.ShapeDtypeStruct((24, 128), F32)
+    half = jax.ShapeDtypeStruct((16, 128), F32)
     kb_from, kb_to = STAGES[stage]
     edges = tile_edges(stage, parts)
     row_from, row_to = edges[0], edges[-1]
@@ -301,13 +338,13 @@
         pltpu.VMEM((row_to - row_from, 2 * pix_count), BF16),
         pltpu.VMEM((GROUPS, 2 * pix_count), F32),
         pltpu.VMEM((16, pix_count), F32),
-        pltpu.VMEM((RIGHT_AT, pix_count), F32),
+        pltpu.VMEM((RIGHT_AT + 4, pix_count), F32),
         pltpu.SemaphoreType.DMA((len(fill),)),
         pltpu.SemaphoreType.DMA((1,)),
     ]
     if late:
         out_shape = [half, half, grads]
-        scratch = [pltpu.VMEM(moments.shape, F32), pltpu.VMEM((48, 128), F32)] + work
+        scratch = [pltpu.VMEM(moments.shape, F32), pltpu.VMEM((32, 128), F32)] + work
     else:
         out_shape = [moments, grads, jax.ShapeDtypeStruct((16, pix_count), BF16)]
         scratch = work
@@ -369,23 +406,26 @@
     )(core, grads, perm)
 
 
-def whiten_kernel(core, own_ref, other_ref, white_ref, score_ref, both, rows, sem):
+def whiten_kernel(core, own_ref, other_ref, weight_ref, white_ref, score_ref, both, rows, sem):
     loads = [
-        pltpu.make_async_copy(ref, both.at[pl.ds(pl.multiple_of(at * 32, 32), 32), :], sem.at[i])
+        pltpu.make_async_copy(ref, both.at[pl.ds(pl.multiple_of(at * 24, 8), 24), :], sem.at[i])
         for i, (ref, at) in enumerate([(own_ref, core[0]), (other_ref, 1 - core[0])])
     ]
     for copy in loads:
         copy.start()
     for copy in loads:
         copy.wait()
-    low = jnp.concatenate([both[0:24, :], both[32:56, :]], axis=0)
+    low = jnp.concatenate([both[0:12, :], both[24:36, :]], axis=0)
     moments = jnp.concatenate([low[:, :GROUPS], low[:, GROUPS:]], axis=0)
+    right = jnp.concatenate([moments[RIGHT_AT:], jnp.zeros((4, GROUPS), F32)], axis=0)
+    moments = jnp.dot(
+        weight_ref[...], moments[: RIGHT_AT + 4], precision=lax.Precision.HIGHEST, preferred_element_type=F32
+    )
     at = 0
     rows[...] = jnp.zeros_like(rows)
     for j in range(ZERN):
         rows[j, j:ZERN, :] = moments[at : at + ZERN - j]
         at += ZERN - j
-    right = moments[RIGHT_AT : RIGHT_AT + 16]
     line = [rows[j] for j in range(ZERN)]
     lane_row = lax.broadcasted_iota(jnp.int32, (16, GROUPS), 0)
     done = jnp.zeros((16, GROUPS), F32)
@@ -399,8 +439,8 @@
             line[i] = line[i] - col[i : i + 1] * col
     white_ref[...] = done[:ZERN]
     for h in range(2):
-        grad = both[32 * h + 24 : 32 * h + 28, :]
-        curv = both[32 * h + 28 : 32 * h + 32, :]
+        grad = both[24 * h + 16 : 24 * h + 20, :]
+        curv = both[24 * h + 20 : 24 * h + 24, :]
         score_ref[4 * h : 4 * h + 4, :] = -grad * lax.rsqrt(curv + 1e-06)
 
 
@@ -418,19 +458,19 @@
     other = lax.ppermute(mine, "pix", CORE_SWAP)
     white, score = pl.pallas_call(
         whiten_kernel,
-        in_specs=[SMEM] + [pl.BlockSpec(memory_space=pl.ANY)] * 2,
+        in_specs=[SMEM] + [pl.BlockSpec(memory_space=pl.ANY)] * 2 + [VMEM],
         out_shape=[
             jax.ShapeDtypeStruct((ZERN, GROUPS), F32),
             jax.ShapeDtypeStruct((8, 128), F32),
         ],
         scratch_shapes=[
-            pltpu.VMEM((64, 128), F32),
+            pltpu.VMEM((48, 128), F32),
             pltpu.VMEM((ZERN, 16, GROUPS), F32),
             pltpu.SemaphoreType.DMA((2,)),
         ],
         compiler_params=params(),
         name="whiten",
-    )(core, mine, other)
+    )(core, mine, other, jnp.asarray(product_weights()))
     return white.T, score.reshape(-1)
 
 

time: 111 us -> 110 us (level)
    unnamed x16 -> x18, local copies, waits for them, and re-layouts: 5.2 us -> 5.2 us
where the time goes in v3:
time: 110 us
  Pallas kernels  31.1 us (28%)
  starting transfers between devices  26.6 us (24%)
  waiting for transfers between devices  23.4 us (21%)
  blocking collectives  19.3 us (18%)
  local copies, waits for them, and re-layouts  7.88 us (7%)
    pallas_call x3, Pallas kernels, particle_terms(): pl.pallas_call(body, in_specs=specs, out_specs=[VMEM] * len(out_shape), o...  19.6 us
    all_to_all x1, blocking collectives, reduce_all(): lax.all_to_all(spread(mine, 16), 'pix', 0, 0, axis_index_groups=CORE_GROUPS)  19.3 us
    ppermute x9, waiting for transfers between devices, hop(): return lax.ppermute(block, 'dom', perm)  17.9 us
    ppermute x9, starting transfers between devices, hop(): return lax.ppermute(block, 'dom', perm)  14.9 us
    pallas_call x1, Pallas kernels, sort_particles(): pl.pallas_call(sort_kernel, grid=(cols // 512,), in_specs=[SMEM, SMEM, ro...  9.86 us
    unnamed x18, local copies, waits for them, and re-layouts  5.2 us
    all_to_all x1, starting transfers between devices, reduce_all(): moments = jnp.sum(lax.all_to_all(spread(mine, 8), 'dom', 0, 0), axis=0)  4.57 us
    ppermute x1, starting transfers between devices, reduce_all(): other = lax.ppermute(mine, 'pix', CORE_SWAP)  3.22 us
  transfers between devices with their start and end apart: 13, of which 9 were waited for; matrix products, arithmetic and copies ran while one was open for 6% of the time, Pallas kernels for 24%

profile of v3, /device:TPU:1, one launch (start us, length us, event | category | flops | bytes accessed | tf_op | source)
XLA Modules:
  0.0 109.8 jit_solution(10361170244797279250)
XLA Ops:
  0.6 1.5 %copy.11 = bf16[32,8,2,1024]{3,1,2,0:T(8,128)(2,1)S(1)} copy(bf16[32,8,2,1024]{3,2,1,0:T(2,128)(2,1)} %bitcast.24) | data formatting | bytes 2097152
  2.1 2.2 %collective-permute-start.1 = (bf16[256,2048]{1,0:T(8,128)(2,1)S(1)}, bf16[256,2048]{1,0:T(8,128)(2,1)S(1)}, u32[]{:S(2)}, u32[]{:S(2)}) collective-permute-start(bf16[256,2048]{1,0:T(8,128)(2,1)S(1)} %bitcast.15), channel_id=1, source_target_pairs={{0,64},{32,96},{64,128},{96,160},{128,192},{160,224},{192,0},{224,... | collective-permute-start | bytes 3145736 | tf_op jit(solution)/shard_map/ppermute | solution.py:478
  4.3 1.2 %collective-permute-start = (bf16[256,2048]{1,0:T(8,128)(2,1)S(1)}, bf16[256,2048]{1,0:T(8,128)(2,1)}, u32[]{:S(2)}, u32[]{:S(2)}) collective-permute-start(bf16[256,2048]{1,0:T(8,128)(2,1)S(1)} %bitcast.16), channel_id=1, source_target_pairs={{0,32},{32,0},{64,96},{96,64},{128,160},{160,128},{192,224},{224,1... | collective-permute-start | bytes 3145736 | tf_op jit(solution)/shard_map/ppermute | solution.py:478
  5.6 1.5 %collective-permute-start.2 = (bf16[256,2048]{1,0:T(8,128)(2,1)S(1)}, bf16[256,2048]{1,0:T(8,128)(2,1)S(1)}, u32[]{:S(2)}, u32[]{:S(2)}) collective-permute-start(bf16[256,2048]{1,0:T(8,128)(2,1)S(1)} %bitcast.17), channel_id=1, source_target_pairs={{0,192},{32,224},{64,0},{96,32},{128,64},{160,96},{192,128},{224,1... | collective-permute-start | bytes 3145736 | tf_op jit(solution)/shard_map/ppermute | solution.py:478
  7.1 3.7 %copy.10 = bf16[128,8,2,1024]{3,1,2,0:T(8,128)(2,1)S(1)} copy(bf16[128,8,2,1024]{3,2,1,0:T(2,128)(2,1)} %bitcast.23) | data formatting | bytes 8388608
  10.9 9.9 %sort_particles.1 = (bf16[1024,2048]{1,0:T(8,128)(2,1)}, bf16[1024,1024]{1,0:T(8,128)(2,1)}, f32[1024,16]{1,0:T(8,128)S(1)}, f32[16,1024]{1,0:T(8,128)S(1)}, s32[9]{0:T(128)S(1)}) custom-call(s32[1]{0:T(128)} %bitcast.2.place, s32[8]{0:T(128)S(1)} %copy-done.6, s32[1,1024]{1,0:T(1,128)S(1)} %bitcast.20, s32[1,1024]{1,0:T(1,128)S(1)} %bitcast.21, ...), custom_call_target="tpu_custom_call" | custom-call | flops 4294967296 | bytes 8388608 | tf_op jit(solution)/shard_map/sort_particles/pallas_call | solution.py:99
  20.7 0.8 slice.81
  21.5 5.2 %collective-permute-done.1.refs_7_ = bf16[256,2048]{1,0:T(8,128)(2,1)S(1)} collective-permute-done((bf16[256,2048]{1,0:T(8,128)(2,1)S(1)}, bf16[256,2048]{1,0:T(8,128)(2,1)S(1)}, u32[]{:S(2)}, u32[]{:S(2)}) %collective-permute-start.1) | collective-permute-done | bytes 1048608 | tf_op jit(solution)/shard_map/ppermute | solution.py:478
  26.7 1.2 %collective-permute-done.refs_6_ = bf16[256,2048]{1,0:T(8,128)(2,1)} collective-permute-done((bf16[256,2048]{1,0:T(8,128)(2,1)S(1)}, bf16[256,2048]{1,0:T(8,128)(2,1)}, u32[]{:S(2)}, u32[]{:S(2)}) %collective-permute-start) | collective-permute-done | bytes 1048608 | tf_op jit(solution)/shard_map/ppermute | solution.py:478
  27.9 1.1 fusion.5
  29.1 1.6 %collective-permute-start.3 = (bf16[512,1024]{1,0:T(8,128)(2,1)S(1)}, bf16[512,1024]{1,0:T(8,128)(2,1)S(1)}, u32[]{:S(2)}, u32[]{:S(2)}) collective-permute-start(bf16[512,1024]{1,0:T(8,128)(2,1)S(1)} %maximum_maximum_fusion), channel_id=1, source_target_pairs={{0,64},{32,96},{64,128},{96,160},{128,192},{160,224},{192,0},{224,... | collective-permute-start | bytes 3145736 | tf_op jit(solution)/shard_map/ppermute | solution.py:478
  30.9 1.2 %collective-permute-start.4 = (bf16[528,1024]{1,0:T(8,128)(2,1)S(1)}, bf16[528,1024]{1,0:T(8,128)(2,1)S(1)}, u32[]{:S(2)}, u32[]{:S(2)}) collective-permute-start(bf16[528,1024]{1,0:T(8,128)(2,1)S(1)} %pad_maximum_fusion), channel_id=1, source_target_pairs={{0,192},{32,224},{64,0},{96,32},{128,64},{160,96},{192,128},{224,1... | collective-permute-start | bytes 3244040 | tf_op jit(solution)/shard_map/ppermute | solution.py:478
  32.3 1.9 %collective-permute-start.5 = (bf16[512,1024]{1,0:T(8,128)(2,1)S(1)}, bf16[512,1024]{1,0:T(8,128)(2,1)S(1)}, u32[]{:S(2)}, u32[]{:S(2)}) collective-permute-start(bf16[512,1024]{1,0:T(8,128)(2,1)S(1)} %maximum_maximum_fusion.1), channel_id=1, source_target_pairs={{0,32},{32,0},{64,96},{96,64},{128,160},{160,128},{192,224},{224,1... | collective-permute-start | bytes 3145736 | tf_op jit(solution)/shard_map/ppermute | solution.py:478
  34.2 8.3 %terms_0.1 = (f32[48,64]{1,0:T(8,128)S(1)}, f32[2,1024]{1,0:T(2,128)S(1)}, bf16[16,1024]{1,0:T(8,128)(2,1)S(1)}) custom-call(s32[1]{0:T(128)} %bitcast.1.refs_0_.refs_1_, s32[9]{0:T(128)S(1)} %get-tuple-element.19.refs_1_.refs_2_, f32[1024,16]{1,0:T(8,128)S(1)} %get-tuple-element.20.refs_2_.refs_3_, f32[16,1024]{1,0:T(8,128)S(1)} %get-tuple-element.21.refs_3_.refs_4_, ...), custom_call_target="tpu_custom_call" | custom-call | flops 17179869184 | bytes 8388608 | tf_op jit(solution)/shard_map/terms_0/pallas_call | solution.py:355
  42.5 10.3 %collective-permute-done.3.refs_7_ = bf16[512,1024]{1,0:T(8,128)(2,1)S(1)} collective-permute-done((bf16[512,1024]{1,0:T(8,128)(2,1)S(1)}, bf16[512,1024]{1,0:T(8,128)(2,1)S(1)}, u32[]{:S(2)}, u32[]{:S(2)}) %collective-permute-start.3) | collective-permute-done | bytes 1048608 | tf_op jit(solution)/shard_map/ppermute | solution.py:478
  52.9 0.7 collective-permute-start.7
  54.3 1.3 %collective-permute-start.6 = (bf16[272,1024]{1,0:T(8,128)(2,1)S(1)}, bf16[272,1024]{1,0:T(8,128)(2,1)S(1)}, u32[]{:S(2)}, u32[]{:S(2)}) collective-permute-start(bf16[272,1024]{1,0:T(8,128)(2,1)S(1)} %pad_maximum_fusion.1), channel_id=1, source_target_pairs={{0,32},{32,0},{64,96},{96,64},{128,160},{160,128},{192,224},{224,1... | collective-permute-start | bytes 1671176 | tf_op jit(solution)/shard_map/ppermute | solution.py:478
  55.6 3.2 %collective-permute-start.8 = (bf16[128,1024]{1,0:T(8,128)(2,1)S(1)}, bf16[128,1024]{1,0:T(8,128)(2,1)S(1)}, u32[]{:S(2)}, u32[]{:S(2)}) collective-permute-start(bf16[128,1024]{1,0:T(8,128)(2,1)S(1)} %get-tuple-element.36), channel_id=1, source_target_pairs={{0,192},{32,224},{64,0},{96,32},{128,64},{160,96},{192,128},{224,1... | collective-permute-start | bytes 786440 | tf_op jit(solution)/shard_map/ppermute | solution.py:478
  58.8 7.7 %terms_1.1 = (f32[48,64]{1,0:T(8,128)S(1)}, f32[2,1024]{1,0:T(2,128)S(1)}, bf16[16,1024]{1,0:T(8,128)(2,1)}) custom-call(s32[1]{0:T(128)} %bitcast.1.refs_0_.refs_1_, s32[9]{0:T(128)S(1)} %get-tuple-element.19.refs_1_.refs_2_, f32[1024,16]{1,0:T(8,128)S(1)} %get-tuple-element.20.refs_2_.refs_3_, f32[16,1024]{1,0:T(8,128)S(1)} %get-tuple-element.21.refs_3_.refs_4_, ...), custom_call_target="tpu_custom_call" | custom-call | flops 12884901888 | bytes 8388608 | tf_op jit(solution)/shard_map/terms_1/pallas_call | solution.py:355
  66.5 0.6 collective-permute-done.6.refs_8_
  67.1 3.6 %terms_2.1 = (f32[16,128]{1,0:T(8,128)S(1)}, f32[16,128]{1,0:T(8,128)S(1)}, f32[2,1024]{1,0:T(2,128)S(1)}) custom-call(s32[1]{0:T(128)} %bitcast.refs_0_.core, s32[1]{0:T(128)} %bitcast.1.refs_0_.refs_1_, s32[9]{0:T(128)S(1)} %get-tuple-element.19.refs_1_.refs_2_, f32[1024,16]{1,0:T(8,128)S(1)} %get-tuple-element.20.refs_2_.refs_3_, ...), custom_call_target="tpu_custom_call" | custom-call | flops 4294967296 | bytes 8388608 | tf_op jit(solution)/shard_map/terms_2/pallas_call | solution.py:355
  70.8 3.2 %collective-permute-start.9 = (f32[16,128]{1,0:T(8,128)S(1)}, f32[16,128]{1,0:T(8,128)S(1)}, u32[]{:S(2)}, u32[]{:S(2)}) collective-permute-start(f32[16,128]{1,0:T(8,128)S(1)} %get-tuple-element.29), channel_id=1, source_target_pairs={{0,1},{1,0},{2,3},{3,2},{4,5},{5,4},{6,7},{7,6},{8,9},{9,8},{10,11... | collective-permute-start | bytes 24584 | tf_op jit(solution)/shard_map/ppermute | solution.py:452
  74.0 0.8 collective-permute-done.9
  74.8 0.6 broadcast_in_dim.27
  75.4 4.6 %all-to-all-start = ((f32[8,16,128]{2,1,0:T(8,128)}), f32[8,16,128]{2,1,0:T(8,128)S(1)}, u32[]{:S(2)}, u32[]{:S(2)}) async-start(f32[8,16,128]{2,1,0:T(8,128)} %broadcast_in_dim.27), calls=%async_computation | async-start | bytes 131072 | tf_op jit(solution)/shard_map/all_to_all | solution.py:453
  80.6 0.7 collective-permute-start.10
  81.3 0.8 collective-permute-done.10
  82.1 3.1 %all-to-all-done = f32[8,16,128]{2,1,0:T(8,128)S(1)} async-done(((f32[8,16,128]{2,1,0:T(8,128)}), f32[8,16,128]{2,1,0:T(8,128)S(1)}, u32[]{:S(2)}, u32[]{:S(2)}) %all-to-all-start) | async-done | bytes 65568 | tf_op jit(solution)/shard_map/all_to_all | solution.py:453
  85.2 19.3 %all_to_all.10 = f32[16,24,128]{2,1,0:T(8,128)S(1)} all-to-all(f32[16,24,128]{2,1,0:T(8,128)S(1)} %broadcast_in_dim.28), channel_id=1, replica_groups={{0,2,4,6,8,10,12,14,16,18,20,22,24,26,28,30},{1,3,5,7,9,11,13,15,17,19,..., dimensions={0} | all-to-all | bytes 393216 | tf_op jit(solution)/shard_map/all_to_all | solution.py:457
  104.6 3.2 %collective-permute-start.11 = (f32[24,128]{1,0:T(8,128)S(1)}, f32[24,128]{1,0:T(8,128)S(1)}, u32[]{:S(2)}, u32[]{:S(2)}) collective-permute-start(f32[24,128]{1,0:T(8,128)S(1)} %reduce_sum.19.own_ref), channel_id=1, source_target_pairs={{0,1},{1,0},{2,3},{3,2},{4,5},{5,4},{6,7},{7,6},{8,9},{9,8},{10,11... | collective-permute-start | bytes 36872 | tf_op jit(solution)/shard_map/ppermute | solution.py:458
  107.8 0.8 collective-permute-done.11.other_ref
  108.7 1.0 whiten.1
  (39 shorter events, 1.9 us)
Async XLA Ops:
  0.6 6.5 %copy-start.7 = (bf16[1024]{0:T(1024)(128)(2,1)S(1)}, bf16[1024]{0:T(1024)(128)(2,1)}, u32[]{:S(2)}) copy-start(bf16[1024]{0:T(1024)(128)(2,1)} %param.13) | copy-start | bytes 6148
  2.1 24.5 %collective-permute-start.1 = (bf16[256,2048]{1,0:T(8,128)(2,1)S(1)}, bf16[256,2048]{1,0:T(8,128)(2,1)S(1)}, u32[]{:S(2)}, u32[]{:S(2)}) collective-permute-start(bf16[256,2048]{1,0:T(8,128)(2,1)S(1)} %bitcast.15), channel_id=1, source_target_pairs={{0,64},{32,96},{64,128},{96,160},{128,192},{160,224},{192,0},{224,... | collective-permute-start | bytes 3145736 | tf_op jit(solution)/shard_map/ppermute | solution.py:478
  4.3 23.5 %collective-permute-start = (bf16[256,2048]{1,0:T(8,128)(2,1)S(1)}, bf16[256,2048]{1,0:T(8,128)(2,1)}, u32[]{:S(2)}, u32[]{:S(2)}) collective-permute-start(bf16[256,2048]{1,0:T(8,128)(2,1)S(1)} %bitcast.16), channel_id=1, source_target_pairs={{0,32},{32,0},{64,96},{96,64},{128,160},{160,128},{192,224},{224,1... | collective-permute-start | bytes 3145736 | tf_op jit(solution)/shard_map/ppermute | solution.py:478
  5.6 25.2 %collective-permute-start.2 = (bf16[256,2048]{1,0:T(8,128)(2,1)S(1)}, bf16[256,2048]{1,0:T(8,128)(2,1)S(1)}, u32[]{:S(2)}, u32[]{:S(2)}) collective-permute-start(bf16[256,2048]{1,0:T(8,128)(2,1)S(1)} %bitcast.17), channel_id=1, source_target_pairs={{0,192},{32,224},{64,0},{96,32},{128,64},{160,96},{192,128},{224,1... | collective-permute-start | bytes 3145736 | tf_op jit(solution)/shard_map/ppermute | solution.py:478
  7.1 3.7 %copy-start.3 = (s32[1024,1]{0,1:T(1,128)S(1)}, s32[1024,1]{0,1:T(1,128)}, u32[]{:S(2)}) copy-start(s32[1024,1]{0,1:T(1,128)} %param.10) | copy-start | bytes 12292
  7.1 3.7 %copy-start.4 = (s32[1024]{0:T(1024)S(1)}, s32[1024]{0:T(1024)}, u32[]{:S(2)}) copy-start(s32[1024]{0:T(1024)} %param.11) | copy-start | bytes 12292
  7.1 3.7 %copy-start.5 = (s32[1024]{0:T(1024)S(1)}, s32[1024]{0:T(1024)}, u32[]{:S(2)}) copy-start(s32[1024]{0:T(1024)} %param.12) | copy-start | bytes 12292
  7.1 3.7 %copy-start.6 = (s32[8]{0:T(128)S(1)}, s32[8]{0:T(128)}, u32[]{:S(2)}) copy-start(s32[8]{0:T(128)} %slot_class.1) | copy-start | bytes 100
  29.1 23.8 %collective-permute-start.3 = (bf16[512,1024]{1,0:T(8,128)(2,1)S(1)}, bf16[512,1024]{1,0:T(8,128)(2,1)S(1)}, u32[]{:S(2)}, u32[]{:S(2)}) collective-permute-start(bf16[512,1024]{1,0:T(8,128)(2,1)S(1)} %maximum_maximum_fusion), channel_id=1, source_target_pairs={{0,64},{32,96},{64,128},{96,160},{128,192},{160,224},{192,0},{224,... | collective-permute-start | bytes 3145736 | tf_op jit(solution)/shard_map/ppermute | solution.py:478
  30.9 3.3 %copy-start.2 = (bf16[1024,2048]{1,0:T(8,128)(2,1)S(1)}, bf16[1024,2048]{1,0:T(8,128)(2,1)}, u32[]{:S(2)}) copy-start(bf16[1024,2048]{1,0:T(8,128)(2,1)} %get-tuple-element.22.refs_4_.refs_6_.refs_7_) | copy-start | bytes 12582916
  30.9 23.3 %collective-permute-start.4 = (bf16[528,1024]{1,0:T(8,128)(2,1)S(1)}, bf16[528,1024]{1,0:T(8,128)(2,1)S(1)}, u32[]{:S(2)}, u32[]{:S(2)}) collective-permute-start(bf16[528,1024]{1,0:T(8,128)(2,1)S(1)} %pad_maximum_fusion), channel_id=1, source_target_pairs={{0,192},{32,224},{64,0},{96,32},{128,64},{160,96},{192,128},{224,1... | collective-permute-start | bytes 3244040 | tf_op jit(solution)/shard_map/ppermute | solution.py:478
  32.3 26.5 %collective-permute-start.5 = (bf16[512,1024]{1,0:T(8,128)(2,1)S(1)}, bf16[512,1024]{1,0:T(8,128)(2,1)S(1)}, u32[]{:S(2)}, u32[]{:S(2)}) collective-permute-start(bf16[512,1024]{1,0:T(8,128)(2,1)S(1)} %maximum_maximum_fusion.1), channel_id=1, source_target_pairs={{0,32},{32,0},{64,96},{96,64},{128,160},{160,128},{192,224},{224,1... | collective-permute-start | bytes 3145736 | tf_op jit(solution)/shard_map/ppermute | solution.py:478
  52.9 13.6 %collective-permute-start.7 = (bf16[128,1024]{1,0:T(8,128)(2,1)S(1)}, bf16[128,1024]{1,0:T(8,128)(2,1)S(1)}, u32[]{:S(2)}, u32[]{:S(2)}) collective-permute-start(bf16[128,1024]{1,0:T(8,128)(2,1)S(1)} %get-tuple-element.38), channel_id=1, source_target_pairs={{0,64},{32,96},{64,128},{96,160},{128,192},{160,224},{192,0},{224,... | collective-permute-start | bytes 786440 | tf_op jit(solution)/shard_map/ppermute | solution.py:478
  54.3 12.9 %collective-permute-start.6 = (bf16[272,1024]{1,0:T(8,128)(2,1)S(1)}, bf16[272,1024]{1,0:T(8,128)(2,1)S(1)}, u32[]{:S(2)}, u32[]{:S(2)}) collective-permute-start(bf16[272,1024]{1,0:T(8,128)(2,1)S(1)} %pad_maximum_fusion.1), channel_id=1, source_target_pairs={{0,32},{32,0},{64,96},{96,64},{128,160},{160,128},{192,224},{224,1... | collective-permute-start | bytes 1671176 | tf_op jit(solution)/shard_map/ppermute | solution.py:478
  55.6 10.9 %collective-permute-start.8 = (bf16[128,1024]{1,0:T(8,128)(2,1)S(1)}, bf16[128,1024]{1,0:T(8,128)(2,1)S(1)}, u32[]{:S(2)}, u32[]{:S(2)}) collective-permute-start(bf16[128,1024]{1,0:T(8,128)(2,1)S(1)} %get-tuple-element.36), channel_id=1, source_target_pairs={{0,192},{32,224},{64,0},{96,32},{128,64},{160,96},{192,128},{224,1... | collective-permute-start | bytes 786440 | tf_op jit(solution)/shard_map/ppermute | solution.py:478
  67.1 12.9 %copy-start = (bf16[1024,1024]{1,0:T(8,128)(2,1)S(1)}, bf16[1024,1024]{1,0:T(8,128)(2,1)}, u32[]{:S(2)}) copy-start(bf16[1024,1024]{1,0:T(8,128)(2,1)} %get-tuple-element.31.perm_ref) | copy-start | bytes 6291460
  70.7 37.9 %copy-start.1 = (f32[80,40]{1,0:T(8,128)S(1)}, f32[80,40]{1,0:T(8,128)}, u32[]{:S(2)}) copy-start(f32[80,40]{1,0:T(8,128)} %constant.17.clone.weight_ref) | copy-start | bytes 38404
  70.8 4.0 %collective-permute-start.9 = (f32[16,128]{1,0:T(8,128)S(1)}, f32[16,128]{1,0:T(8,128)S(1)}, u32[]{:S(2)}, u32[]{:S(2)}) collective-permute-start(f32[16,128]{1,0:T(8,128)S(1)} %get-tuple-element.29), channel_id=1, source_target_pairs={{0,1},{1,0},{2,3},{3,2},{4,5},{5,4},{6,7},{7,6},{8,9},{9,8},{10,11... | collective-permute-start | bytes 24584 | tf_op jit(solution)/shard_map/ppermute | solution.py:452
  75.4 9.8 %all-to-all-start = ((f32[8,16,128]{2,1,0:T(8,128)}), f32[8,16,128]{2,1,0:T(8,128)S(1)}, u32[]{:S(2)}, u32[]{:S(2)}) async-start(f32[8,16,128]{2,1,0:T(8,128)} %broadcast_in_dim.27), calls=%async_computation | async-start | bytes 131072 | tf_op jit(solution)/shard_map/all_to_all | solution.py:453
  80.6 1.5 %collective-permute-start.10 = (f32[8,128]{1,0:T(8,128)S(1)}, f32[8,128]{1,0:T(8,128)S(1)}, u32[]{:S(2)}, u32[]{:S(2)}) collective-permute-start(f32[8,128]{1,0:T(8,128)S(1)} %get-tuple-element.33), channel_id=1, source_target_pairs={{0,1},{1,0},{2,3},{3,2},{4,5},{5,4},{6,7},{7,6},{8,9},{9,8},{10,11... | collective-permute-start | bytes 12296 | tf_op jit(solution)/shard_map/ppermute | solution.py:455
  104.6 4.1 %collective-permute-start.11 = (f32[24,128]{1,0:T(8,128)S(1)}, f32[24,128]{1,0:T(8,128)S(1)}, u32[]{:S(2)}, u32[]{:S(2)}) collective-permute-start(f32[24,128]{1,0:T(8,128)S(1)} %reduce_sum.19.own_ref), channel_id=1, source_target_pairs={{0,1},{1,0},{2,3},{3,2},{4,5},{5,4},{6,7},{7,6},{8,9},{9,8},{10,11... | collective-permute-start | bytes 36872 | tf_op jit(solution)/shard_map/ppermute | solution.py:458

commit v4 on v3

--- a/solution.py
+++ b/solution.py
@@ -528,16 +528,16 @@
         images.reshape(parts, 2 * pix_count),
     )
 
-    up = hop(rows(part_a(side), part_a(below[:128]), part_b(below[:128])), Y_UP)
-    down = hop(rows(part_a(side), part_a(above[128:]), part_b(above[128:]), image_rows[:16, :pix_count]), Y_DOWN)
+    up = hop(rows(part_a(side), part_a(below[:128]), part_b(below[:128]), image_rows[:16, :pix_count]), Y_UP)
+    down = hop(rows(part_a(side), part_a(above[128:]), part_b(above[128:])), Y_DOWN)
     b_side = hop(rows(part_b(below), part_b(above)), X_SWAP)
     fill = fills(pix_count)
     shared = (first, counts, mark_cols, mark_rows, image_rows)
     *sums, token = particle_terms(0, fill[0], *shared, [flat, side, below, above])
 
-    far_a_0 = hop(up[:128], Y_UP)
+    far_a_0 = hop(rows(up[:128], token), Y_UP)
     far_a_1 = hop(down[128:256], Y_DOWN)
-    far_b = hop(rows(up[384:512], down[384:512], token), X_SWAP)
+    far_b = hop(rows(up[384:512], down[384:512]), X_SWAP)
     *sums, _ = particle_terms(1, fill[1], *shared, [up, down, b_side], sums)
     keep, send, grads = particle_terms(2, fill[2], *shared, [far_b, far_a_0, far_a_1], sums, core)
     return reduce_all(core, keep, send, grads, perm)

time: 110 us -> 110 us (level)
  Pallas kernels: 31.1 us -> 34 us
  starting transfers between devices: 26.6 us -> 24.8 us
  waiting for transfers between devices: 23.4 us -> 21.7 us
    pallas_call x3, Pallas kernels: 19.6 us -> 22.6 us  [particle_terms(): pl.pallas_call(body, in_specs=specs, out_specs=[VMEM] * len(out_shape), o...]
    ppermute x9, waiting for transfers between devices: 17.9 us -> 15.7 us  [hop(): return lax.ppermute(block, 'dom', perm)]
    all_to_all x1, starting transfers between devices: 4.57 us -> 3.35 us  [reduce_all(): moments = jnp.sum(lax.all_to_all(spread(mine, 8), 'dom', 0, 0), axis=0)]
  transfers between devices with their start and end apart: 13 -> 13, of which waited for: 9 -> 8; matrix products, arithmetic and copies ran while one was open for 6% -> 6% of each run, Pallas kernels for 24% -> 27%
where the time goes in v4:
time: 110 us
  Pallas kernels  34 us (31%)
  starting transfers between devices  24.8 us (23%)
  waiting for transfers between devices  21.7 us (20%)
  blocking collectives  19.8 us (18%)
  local copies, waits for them, and re-layouts  7.88 us (7%)
    pallas_call x3, Pallas kernels, particle_terms(): pl.pallas_call(body, in_specs=specs, out_specs=[VMEM] * len(out_shape), o...  22.6 us
    all_to_all x1, blocking collectives, reduce_all(): lax.all_to_all(spread(mine, 16), 'pix', 0, 0, axis_index_groups=CORE_GROUPS)  19.8 us
    ppermute x9, waiting for transfers between devices, hop(): return lax.ppermute(block, 'dom', perm)  15.7 us
    ppermute x9, starting transfers between devices, hop(): return lax.ppermute(block, 'dom', perm)  14.4 us
    pallas_call x1, Pallas kernels, sort_particles(): pl.pallas_call(sort_kernel, grid=(cols // 512,), in_specs=[SMEM, SMEM, ro...  9.86 us
    unnamed x18, local copies, waits for them, and re-layouts  5.2 us
    ppermute x1, starting transfers between devices, reduce_all(): mine = keep + lax.ppermute(send, 'pix', CORE_SWAP)  3.75 us
    all_to_all x1, waiting for transfers between devices, reduce_all(): moments = jnp.sum(lax.all_to_all(spread(mine, 8), 'dom', 0, 0), axis=0)  3.45 us
  transfers between devices with their start and end apart: 13, of which 8 were waited for; matrix products, arithmetic and copies ran while one was open for 6% of the time, Pallas kernels for 27%

profile of v4, /device:TPU:1, one launch (start us, length us, event | category | flops | bytes accessed | tf_op | source)
XLA Modules:
  0.0 109.7 jit_solution(18350517760220358558)
XLA Ops:
  0.6 1.5 %copy.11 = bf16[32,8,2,1024]{3,1,2,0:T(8,128)(2,1)S(1)} copy(bf16[32,8,2,1024]{3,2,1,0:T(2,128)(2,1)} %bitcast.24) | data formatting | bytes 2097152
  2.1 2.2 %collective-permute-start.1 = (bf16[256,2048]{1,0:T(8,128)(2,1)S(1)}, bf16[256,2048]{1,0:T(8,128)(2,1)S(1)}, u32[]{:S(2)}, u32[]{:S(2)}) collective-permute-start(bf16[256,2048]{1,0:T(8,128)(2,1)S(1)} %bitcast.15), channel_id=1, source_target_pairs={{0,64},{32,96},{64,128},{96,160},{128,192},{160,224},{192,0},{224,... | collective-permute-start | bytes 3145736 | tf_op jit(solution)/shard_map/ppermute | solution.py:478
  4.3 1.2 %collective-permute-start = (bf16[256,2048]{1,0:T(8,128)(2,1)S(1)}, bf16[256,2048]{1,0:T(8,128)(2,1)}, u32[]{:S(2)}, u32[]{:S(2)}) collective-permute-start(bf16[256,2048]{1,0:T(8,128)(2,1)S(1)} %bitcast.16), channel_id=1, source_target_pairs={{0,32},{32,0},{64,96},{96,64},{128,160},{160,128},{192,224},{224,1... | collective-permute-start | bytes 3145736 | tf_op jit(solution)/shard_map/ppermute | solution.py:478
  5.6 1.5 %collective-permute-start.2 = (bf16[256,2048]{1,0:T(8,128)(2,1)S(1)}, bf16[256,2048]{1,0:T(8,128)(2,1)S(1)}, u32[]{:S(2)}, u32[]{:S(2)}) collective-permute-start(bf16[256,2048]{1,0:T(8,128)(2,1)S(1)} %bitcast.17), channel_id=1, source_target_pairs={{0,192},{32,224},{64,0},{96,32},{128,64},{160,96},{192,128},{224,1... | collective-permute-start | bytes 3145736 | tf_op jit(solution)/shard_map/ppermute | solution.py:478
  7.1 3.7 %copy.10 = bf16[128,8,2,1024]{3,1,2,0:T(8,128)(2,1)S(1)} copy(bf16[128,8,2,1024]{3,2,1,0:T(2,128)(2,1)} %bitcast.23) | data formatting | bytes 8388608
  10.9 9.9 %sort_particles.1 = (bf16[1024,2048]{1,0:T(8,128)(2,1)}, bf16[1024,1024]{1,0:T(8,128)(2,1)}, f32[1024,16]{1,0:T(8,128)S(1)}, f32[16,1024]{1,0:T(8,128)S(1)}, s32[9]{0:T(128)S(1)}) custom-call(s32[1]{0:T(128)} %bitcast.2.place, s32[8]{0:T(128)S(1)} %copy-done.6, s32[1,1024]{1,0:T(1,128)S(1)} %bitcast.20, s32[1,1024]{1,0:T(1,128)S(1)} %bitcast.21, ...), custom_call_target="tpu_custom_call" | custom-call | flops 4294967296 | bytes 8388608 | tf_op jit(solution)/shard_map/sort_particles/pallas_call | solution.py:99
  20.7 0.8 slice.77
  21.5 5.2 %collective-permute-done.1.refs_7_ = bf16[256,2048]{1,0:T(8,128)(2,1)S(1)} collective-permute-done((bf16[256,2048]{1,0:T(8,128)(2,1)S(1)}, bf16[256,2048]{1,0:T(8,128)(2,1)S(1)}, u32[]{:S(2)}, u32[]{:S(2)}) %collective-permute-start.1) | collective-permute-done | bytes 1048608 | tf_op jit(solution)/shard_map/ppermute | solution.py:478
  26.7 1.2 %collective-permute-done.refs_6_ = bf16[256,2048]{1,0:T(8,128)(2,1)} collective-permute-done((bf16[256,2048]{1,0:T(8,128)(2,1)S(1)}, bf16[256,2048]{1,0:T(8,128)(2,1)}, u32[]{:S(2)}, u32[]{:S(2)}) %collective-permute-start) | collective-permute-done | bytes 1048608 | tf_op jit(solution)/shard_map/ppermute | solution.py:478
  27.9 1.1 fusion.5
  29.1 1.6 %collective-permute-start.3 = (bf16[528,1024]{1,0:T(8,128)(2,1)S(1)}, bf16[528,1024]{1,0:T(8,128)(2,1)S(1)}, u32[]{:S(2)}, u32[]{:S(2)}) collective-permute-start(bf16[528,1024]{1,0:T(8,128)(2,1)S(1)} %pad_maximum_fusion), channel_id=1, source_target_pairs={{0,64},{32,96},{64,128},{96,160},{128,192},{160,224},{192,0},{224,... | collective-permute-start | bytes 3244040 | tf_op jit(solution)/shard_map/ppermute | solution.py:478
  30.9 1.2 %collective-permute-start.4 = (bf16[512,1024]{1,0:T(8,128)(2,1)S(1)}, bf16[512,1024]{1,0:T(8,128)(2,1)S(1)}, u32[]{:S(2)}, u32[]{:S(2)}) collective-permute-start(bf16[512,1024]{1,0:T(8,128)(2,1)S(1)} %maximum_maximum_fusion), channel_id=1, source_target_pairs={{0,192},{32,224},{64,0},{96,32},{128,64},{160,96},{192,128},{224,1... | collective-permute-start | bytes 3145736 | tf_op jit(solution)/shard_map/ppermute | solution.py:478
  32.4 1.9 %collective-permute-start.5 = (bf16[512,1024]{1,0:T(8,128)(2,1)S(1)}, bf16[512,1024]{1,0:T(8,128)(2,1)S(1)}, u32[]{:S(2)}, u32[]{:S(2)}) collective-permute-start(bf16[512,1024]{1,0:T(8,128)(2,1)S(1)} %maximum_maximum_fusion.1), channel_id=1, source_target_pairs={{0,32},{32,0},{64,96},{96,64},{128,160},{160,128},{192,224},{224,1... | collective-permute-start | bytes 3145736 | tf_op jit(solution)/shard_map/ppermute | solution.py:478
  34.2 11.3 %terms_0.1 = (f32[48,64]{1,0:T(8,128)S(1)}, f32[2,1024]{1,0:T(2,128)S(1)}, bf16[16,1024]{1,0:T(8,128)(2,1)S(1)}) custom-call(s32[1]{0:T(128)} %bitcast.1.refs_0_.refs_1_, s32[9]{0:T(128)S(1)} %get-tuple-element.19.refs_1_.refs_2_, f32[1024,16]{1,0:T(8,128)S(1)} %get-tuple-element.20.refs_2_.refs_3_, f32[16,1024]{1,0:T(8,128)S(1)} %get-tuple-element.21.refs_3_.refs_4_, ...), custom_call_target="tpu_custom_call" | custom-call | flops 17179869184 | bytes 8388608 | tf_op jit(solution)/shard_map/terms_0/pallas_call | solution.py:355
  45.5 8.0 %collective-permute-done.4.refs_8_ = bf16[512,1024]{1,0:T(8,128)(2,1)S(1)} collective-permute-done((bf16[512,1024]{1,0:T(8,128)(2,1)S(1)}, bf16[512,1024]{1,0:T(8,128)(2,1)S(1)}, u32[]{:S(2)}, u32[]{:S(2)}) %collective-permute-start.4) | collective-permute-done | bytes 1048608 | tf_op jit(solution)/shard_map/ppermute | solution.py:478
  53.6 2.1 %collective-permute-start.8 = (bf16[128,1024]{1,0:T(8,128)(2,1)S(1)}, bf16[128,1024]{1,0:T(8,128)(2,1)S(1)}, u32[]{:S(2)}, u32[]{:S(2)}) collective-permute-start(bf16[128,1024]{1,0:T(8,128)(2,1)S(1)} %get-tuple-element.38), channel_id=1, source_target_pairs={{0,192},{32,224},{64,0},{96,32},{128,64},{160,96},{192,128},{224,1... | collective-permute-start | bytes 786440 | tf_op jit(solution)/shard_map/ppermute | solution.py:478
  55.8 2.5 %collective-permute-start.6 = (bf16[256,1024]{1,0:T(8,128)(2,1)S(1)}, bf16[256,1024]{1,0:T(8,128)(2,1)S(1)}, u32[]{:S(2)}, u32[]{:S(2)}) collective-permute-start(bf16[256,1024]{1,0:T(8,128)(2,1)S(1)} %pad_maximum_fusion.1), channel_id=1, source_target_pairs={{0,32},{32,0},{64,96},{96,64},{128,160},{160,128},{192,224},{224,1... | collective-permute-start | bytes 1572872 | tf_op jit(solution)/shard_map/ppermute | solution.py:478
  58.4 7.7 %terms_1.1 = (f32[48,64]{1,0:T(8,128)S(1)}, f32[2,1024]{1,0:T(2,128)S(1)}, bf16[16,1024]{1,0:T(8,128)(2,1)}) custom-call(s32[1]{0:T(128)} %bitcast.1.refs_0_.refs_1_, s32[9]{0:T(128)S(1)} %get-tuple-element.19.refs_1_.refs_2_, f32[1024,16]{1,0:T(8,128)S(1)} %get-tuple-element.20.refs_2_.refs_3_, f32[16,1024]{1,0:T(8,128)S(1)} %get-tuple-element.21.refs_3_.refs_4_, ...), custom_call_target="tpu_custom_call" | custom-call | flops 12884901888 | bytes 8388608 | tf_op jit(solution)/shard_map/terms_1/pallas_call | solution.py:355
  66.1 1.3 %collective-permute-done.6.refs_8_ = bf16[256,1024]{1,0:T(8,128)(2,1)S(1)} collective-permute-done((bf16[256,1024]{1,0:T(8,128)(2,1)S(1)}, bf16[256,1024]{1,0:T(8,128)(2,1)S(1)}, u32[]{:S(2)}, u32[]{:S(2)}) %collective-permute-start.6) | collective-permute-done | bytes 524320 | tf_op jit(solution)/shard_map/ppermute | solution.py:478
  67.5 3.6 %terms_2.1 = (f32[16,128]{1,0:T(8,128)S(1)}, f32[16,128]{1,0:T(8,128)S(1)}, f32[2,1024]{1,0:T(2,128)S(1)}) custom-call(s32[1]{0:T(128)} %bitcast.refs_0_.core, s32[1]{0:T(128)} %bitcast.1.refs_0_.refs_1_, s32[9]{0:T(128)S(1)} %get-tuple-element.19.refs_1_.refs_2_, f32[1024,16]{1,0:T(8,128)S(1)} %get-tuple-element.20.refs_2_.refs_3_, ...), custom_call_target="tpu_custom_call" | custom-call | flops 4294967296 | bytes 8388608 | tf_op jit(solution)/shard_map/terms_2/pallas_call | solution.py:355
  71.1 3.8 %collective-permute-start.9 = (f32[16,128]{1,0:T(8,128)S(1)}, f32[16,128]{1,0:T(8,128)S(1)}, u32[]{:S(2)}, u32[]{:S(2)}) collective-permute-start(f32[16,128]{1,0:T(8,128)S(1)} %get-tuple-element.29), channel_id=1, source_target_pairs={{0,1},{1,0},{2,3},{3,2},{4,5},{5,4},{6,7},{7,6},{8,9},{9,8},{10,11... | collective-permute-start | bytes 24584 | tf_op jit(solution)/shard_map/ppermute | solution.py:452
  74.8 0.8 collective-permute-done.9
  75.7 0.6 broadcast_in_dim.27
  76.3 3.3 %all-to-all-start = ((f32[8,16,128]{2,1,0:T(8,128)}), f32[8,16,128]{2,1,0:T(8,128)S(1)}, u32[]{:S(2)}, u32[]{:S(2)}) async-start(f32[8,16,128]{2,1,0:T(8,128)} %broadcast_in_dim.27), calls=%async_computation | async-start | bytes 131072 | tf_op jit(solution)/shard_map/all_to_all | solution.py:453
  79.7 0.6 unsort.1
  80.3 0.4 collective-permute-start.10
  80.7 0.8 collective-permute-done.10
  81.5 3.5 %all-to-all-done = f32[8,16,128]{2,1,0:T(8,128)S(1)} async-done(((f32[8,16,128]{2,1,0:T(8,128)}), f32[8,16,128]{2,1,0:T(8,128)S(1)}, u32[]{:S(2)}, u32[]{:S(2)}) %all-to-all-start) | async-done | bytes 65568 | tf_op jit(solution)/shard_map/all_to_all | solution.py:453
  85.0 19.8 %all_to_all.10 = f32[16,24,128]{2,1,0:T(8,128)S(1)} all-to-all(f32[16,24,128]{2,1,0:T(8,128)S(1)} %broadcast_in_dim.28), channel_id=1, replica_groups={{0,2,4,6,8,10,12,14,16,18,20,22,24,26,28,30},{1,3,5,7,9,11,13,15,17,19,..., dimensions={0} | all-to-all | bytes 393216 | tf_op jit(solution)/shard_map/all_to_all | solution.py:457
  104.8 2.9 %collective-permute-start.11 = (f32[24,128]{1,0:T(8,128)S(1)}, f32[24,128]{1,0:T(8,128)S(1)}, u32[]{:S(2)}, u32[]{:S(2)}) collective-permute-start(f32[24,128]{1,0:T(8,128)S(1)} %reduce_sum.19.own_ref), channel_id=1, source_target_pairs={{0,1},{1,0},{2,3},{3,2},{4,5},{5,4},{6,7},{7,6},{8,9},{9,8},{10,11... | collective-permute-start | bytes 36872 | tf_op jit(solution)/shard_map/ppermute | solution.py:458
  107.7 0.8 collective-permute-done.11.other_ref
  108.6 1.0 whiten.1
  (40 shorter events, 0.9 us)
Async XLA Ops:
  0.6 6.5 %copy-start.7 = (bf16[1024]{0:T(1024)(128)(2,1)S(1)}, bf16[1024]{0:T(1024)(128)(2,1)}, u32[]{:S(2)}) copy-start(bf16[1024]{0:T(1024)(128)(2,1)} %param.13) | copy-start | bytes 6148
  2.1 24.5 %collective-permute-start.1 = (bf16[256,2048]{1,0:T(8,128)(2,1)S(1)}, bf16[256,2048]{1,0:T(8,128)(2,1)S(1)}, u32[]{:S(2)}, u32[]{:S(2)}) collective-permute-start(bf16[256,2048]{1,0:T(8,128)(2,1)S(1)} %bitcast.15), channel_id=1, source_target_pairs={{0,64},{32,96},{64,128},{96,160},{128,192},{160,224},{192,0},{224,... | collective-permute-start | bytes 3145736 | tf_op jit(solution)/shard_map/ppermute | solution.py:478
  4.3 23.5 %collective-permute-start = (bf16[256,2048]{1,0:T(8,128)(2,1)S(1)}, bf16[256,2048]{1,0:T(8,128)(2,1)}, u32[]{:S(2)}, u32[]{:S(2)}) collective-permute-start(bf16[256,2048]{1,0:T(8,128)(2,1)S(1)} %bitcast.16), channel_id=1, source_target_pairs={{0,32},{32,0},{64,96},{96,64},{128,160},{160,128},{192,224},{224,1... | collective-permute-start | bytes 3145736 | tf_op jit(solution)/shard_map/ppermute | solution.py:478
  5.6 25.2 %collective-permute-start.2 = (bf16[256,2048]{1,0:T(8,128)(2,1)S(1)}, bf16[256,2048]{1,0:T(8,128)(2,1)S(1)}, u32[]{:S(2)}, u32[]{:S(2)}) collective-permute-start(bf16[256,2048]{1,0:T(8,128)(2,1)S(1)} %bitcast.17), channel_id=1, source_target_pairs={{0,192},{32,224},{64,0},{96,32},{128,64},{160,96},{192,128},{224,1... | collective-permute-start | bytes 3145736 | tf_op jit(solution)/shard_map/ppermute | solution.py:478
  7.1 3.7 %copy-start.3 = (s32[1024,1]{0,1:T(1,128)S(1)}, s32[1024,1]{0,1:T(1,128)}, u32[]{:S(2)}) copy-start(s32[1024,1]{0,1:T(1,128)} %param.10) | copy-start | bytes 12292
  7.1 3.7 %copy-start.4 = (s32[1024]{0:T(1024)S(1)}, s32[1024]{0:T(1024)}, u32[]{:S(2)}) copy-start(s32[1024]{0:T(1024)} %param.11) | copy-start | bytes 12292
  7.1 3.7 %copy-start.5 = (s32[1024]{0:T(1024)S(1)}, s32[1024]{0:T(1024)}, u32[]{:S(2)}) copy-start(s32[1024]{0:T(1024)} %param.12) | copy-start | bytes 12292
  7.1 3.7 %copy-start.6 = (s32[8]{0:T(128)S(1)}, s32[8]{0:T(128)}, u32[]{:S(2)}) copy-start(s32[8]{0:T(128)} %slot_class.1) | copy-start | bytes 100
  29.1 26.6 %collective-permute-start.3 = (bf16[528,1024]{1,0:T(8,128)(2,1)S(1)}, bf16[528,1024]{1,0:T(8,128)(2,1)S(1)}, u32[]{:S(2)}, u32[]{:S(2)}) collective-permute-start(bf16[528,1024]{1,0:T(8,128)(2,1)S(1)} %pad_maximum_fusion), channel_id=1, source_target_pairs={{0,64},{32,96},{64,128},{96,160},{128,192},{160,224},{192,0},{224,... | collective-permute-start | bytes 3244040 | tf_op jit(solution)/shard_map/ppermute | solution.py:478
  30.9 3.3 %copy-start.2 = (bf16[1024,2048]{1,0:T(8,128)(2,1)S(1)}, bf16[1024,2048]{1,0:T(8,128)(2,1)}, u32[]{:S(2)}) copy-start(bf16[1024,2048]{1,0:T(8,128)(2,1)} %get-tuple-element.22.refs_4_.refs_6_.refs_7_) | copy-start | bytes 12582916
  30.9 22.6 %collective-permute-start.4 = (bf16[512,1024]{1,0:T(8,128)(2,1)S(1)}, bf16[512,1024]{1,0:T(8,128)(2,1)S(1)}, u32[]{:S(2)}, u32[]{:S(2)}) collective-permute-start(bf16[512,1024]{1,0:T(8,128)(2,1)S(1)} %maximum_maximum_fusion), channel_id=1, source_target_pairs={{0,192},{32,224},{64,0},{96,32},{128,64},{160,96},{192,128},{224,1... | collective-permute-start | bytes 3145736 | tf_op jit(solution)/shard_map/ppermute | solution.py:478
  32.4 26.0 %collective-permute-start.5 = (bf16[512,1024]{1,0:T(8,128)(2,1)S(1)}, bf16[512,1024]{1,0:T(8,128)(2,1)S(1)}, u32[]{:S(2)}, u32[]{:S(2)}) collective-permute-start(bf16[512,1024]{1,0:T(8,128)(2,1)S(1)} %maximum_maximum_fusion.1), channel_id=1, source_target_pairs={{0,32},{32,0},{64,96},{96,64},{128,160},{160,128},{192,224},{224,1... | collective-permute-start | bytes 3145736 | tf_op jit(solution)/shard_map/ppermute | solution.py:478
  53.6 12.5 %collective-permute-start.8 = (bf16[128,1024]{1,0:T(8,128)(2,1)S(1)}, bf16[128,1024]{1,0:T(8,128)(2,1)S(1)}, u32[]{:S(2)}, u32[]{:S(2)}) collective-permute-start(bf16[128,1024]{1,0:T(8,128)(2,1)S(1)} %get-tuple-element.38), channel_id=1, source_target_pairs={{0,192},{32,224},{64,0},{96,32},{128,64},{160,96},{192,128},{224,1... | collective-permute-start | bytes 786440 | tf_op jit(solution)/shard_map/ppermute | solution.py:478
  55.8 11.7 %collective-permute-start.6 = (bf16[256,1024]{1,0:T(8,128)(2,1)S(1)}, bf16[256,1024]{1,0:T(8,128)(2,1)S(1)}, u32[]{:S(2)}, u32[]{:S(2)}) collective-permute-start(bf16[256,1024]{1,0:T(8,128)(2,1)S(1)} %pad_maximum_fusion.1), channel_id=1, source_target_pairs={{0,32},{32,0},{64,96},{96,64},{128,160},{160,128},{192,224},{224,1... | collective-permute-start | bytes 1572872 | tf_op jit(solution)/shard_map/ppermute | solution.py:478
  58.3 7.8 %collective-permute-start.7 = (bf16[144,1024]{1,0:T(8,128)(2,1)S(1)}, bf16[144,1024]{1,0:T(8,128)(2,1)S(1)}, u32[]{:S(2)}, u32[]{:S(2)}) collective-permute-start(bf16[144,1024]{1,0:T(8,128)(2,1)S(1)} %pad_maximum_fusion.2), channel_id=1, source_target_pairs={{0,64},{32,96},{64,128},{96,160},{128,192},{160,224},{192,0},{224,... | collective-permute-start | bytes 884744 | tf_op jit(solution)/shard_map/ppermute | solution.py:478
  67.5 12.2 %copy-start = (bf16[1024,1024]{1,0:T(8,128)(2,1)S(1)}, bf16[1024,1024]{1,0:T(8,128)(2,1)}, u32[]{:S(2)}) copy-start(bf16[1024,1024]{1,0:T(8,128)(2,1)} %get-tuple-element.31.perm_ref) | copy-start | bytes 6291460
  71.1 37.5 %copy-start.1 = (f32[80,40]{1,0:T(8,128)S(1)}, f32[80,40]{1,0:T(8,128)}, u32[]{:S(2)}) copy-start(f32[80,40]{1,0:T(8,128)} %constant.17.clone.weight_ref) | copy-start | bytes 38404
  71.1 4.6 %collective-permute-start.9 = (f32[16,128]{1,0:T(8,128)S(1)}, f32[16,128]{1,0:T(8,128)S(1)}, u32[]{:S(2)}, u32[]{:S(2)}) collective-permute-start(f32[16,128]{1,0:T(8,128)S(1)} %get-tuple-element.29), channel_id=1, source_target_pairs={{0,1},{1,0},{2,3},{3,2},{4,5},{5,4},{6,7},{7,6},{8,9},{9,8},{10,11... | collective-permute-start | bytes 24584 | tf_op jit(solution)/shard_map/ppermute | solution.py:452
  76.3 8.7 %all-to-all-start = ((f32[8,16,128]{2,1,0:T(8,128)}), f32[8,16,128]{2,1,0:T(8,128)S(1)}, u32[]{:S(2)}, u32[]{:S(2)}) async-start(f32[8,16,128]{2,1,0:T(8,128)} %broadcast_in_dim.27), calls=%async_computation | async-start | bytes 131072 | tf_op jit(solution)/shard_map/all_to_all | solution.py:453
  80.3 1.3 %collective-permute-start.10 = (f32[8,128]{1,0:T(8,128)S(1)}, f32[8,128]{1,0:T(8,128)S(1)}, u32[]{:S(2)}, u32[]{:S(2)}) collective-permute-start(f32[8,128]{1,0:T(8,128)S(1)} %get-tuple-element.33), channel_id=1, source_target_pairs={{0,1},{1,0},{2,3},{3,2},{4,5},{5,4},{6,7},{7,6},{8,9},{9,8},{10,11... | collective-permute-start | bytes 12296 | tf_op jit(solution)/shard_map/ppermute | solution.py:455
  104.8 3.7 %collective-permute-start.11 = (f32[24,128]{1,0:T(8,128)S(1)}, f32[24,128]{1,0:T(8,128)S(1)}, u32[]{:S(2)}, u32[]{:S(2)}) collective-permute-start(f32[24,128]{1,0:T(8,128)S(1)} %reduce_sum.19.own_ref), channel_id=1, source_target_pairs={{0,1},{1,0},{2,3},{3,2},{4,5},{5,4},{6,7},{7,6},{8,9},{9,8},{10,11... | collective-permute-start | bytes 36872 | tf_op jit(solution)/shard_map/ppermute | solution.py:458
